TPU v7x, 32 devices: a whole 2x2x4 slice. The times are simulated.
32 devices in a mesh: seq: 8 (over z, core), head: 4 (over y, x).
Axes of the slice: x: 2, y: 2, z: 4, core: 2. Of those that a mesh axis runs over, the one named last changes fastest.
Arguments:
- projections: bfloat16 [6144, 8, 384], P(('seq', 'head')), may hold values from -8 to 8
- routed_heads: int32 [6144, 8], P(('seq', 'head')), may hold values from 0 to 63, as said below
- slot_index: int32 [6144, 8], P(('seq', 'head')), may hold values from 0 to 47, as said below
- gate_logits: float32 [6144, 8], P(('seq', 'head')), may hold values from -8 to 8
- doc_lengths: int32 [16], replicated, may hold values from 1 to 768, 6144 in all
- cotangent: bfloat16 [6144, 8, 128], P(('seq', 'head')), may hold values from -6 to 6
Outputs:
- head_outputs: bfloat16 [6144, 8, 128], P(('seq', 'head'))
- projection_grads: bfloat16 [6144, 8, 384], P(('seq', 'head'))
- gate_grads: float32 [6144, 8], P(('seq', 'head'))
Inputs may be any that keep to these rules, and one draw needn't show every extreme that they name: `routed_heads`: each token names 8 different heads. Among the 192 tokens of one aligned block at most 48 name the same head, and in every aligned run of 768 tokens one head is named by exactly 48 tokens of each of its aligned blocks of 192. slot_index[t, k] is the number of tokens before t in t's aligned block of 192 tokens that name head routed_heads[t, k]. `doc_lengths`: the documents lie in order and together fill the 6144 positions.
All inputs are finite; a program needn't handle non-finite values.
Results may differ from a plain program's by a relative error of at most 0.011.
Values may be sent and summed in bfloat16 or wider, within the bound.
No kernel may reach another device: no remote copies, remote signals or barrier semaphores. Data moves between devices by JAX's collectives and lax.ppermute only.
A program may use at most 64 MiB of HBM per device.

v0:
```python
from functools import partial

import jax
import jax.numpy as jnp
from jax import lax
from jax.sharding import PartitionSpec as P

H = 64
CAP = 48


MASKED = -1e30


def shifted(block, axis, distance):
    devices = range(lax.axis_size(axis))
    route = [(i - distance, i) for i in devices if i - distance in devices]
    return lax.ppermute(block, axis, route)


def visible_pairs(query_docs, key_docs):
    slot_span = query_docs.shape[0]
    row_index = jnp.arange(slot_span, dtype=jnp.int32)[:, None]
    col_index = jnp.arange(key_docs.shape[0], dtype=jnp.int32)[None, :]
    same_doc = (key_docs[None, :] == query_docs[:, None]) & (key_docs[None, :] > 0)
    return same_doc & (col_index - slot_span <= row_index)


def masked_scores(queries, key_rows, visible):
    scaling = queries.shape[1] ** (-0.5)
    scores = jnp.dot(queries, key_rows.T, preferred_element_type=jnp.float32) * scaling
    return jnp.where(visible, scores, MASKED)


def forward_head(operands):
    queries, key_rows, value_rows, query_docs, key_docs = operands
    scores = masked_scores(queries, key_rows, visible_pairs(query_docs, key_docs))
    row_max = jnp.max(scores, axis=1, keepdims=True)
    powers = jnp.exp(scores - row_max)
    row_sum = jnp.sum(powers, axis=1, keepdims=True)
    weights_low = (powers / row_sum).astype(jnp.bfloat16)
    attended = jnp.dot(weights_low, value_rows, preferred_element_type=jnp.float32).astype(
        jnp.bfloat16
    )
    attended = lax.optimization_barrier(attended)
    return (attended, row_max[:, 0], row_sum[:, 0])


def weight_terms(queries, key_rows, value_rows, visible, row_max, row_sum, grads_out, deltas):
    scores = masked_scores(queries, key_rows, visible)
    weights = jnp.exp(scores - row_max[:, None]) / row_sum[:, None]
    weight_grads = jnp.dot(grads_out, value_rows.T, preferred_element_type=jnp.float32)
    score_grads = (weights * (weight_grads - deltas[:, None])).astype(jnp.bfloat16)
    return (weights.astype(jnp.bfloat16), score_grads)


def backward_head(operands, keep_earlier):
    queries, key_rows, value_rows, query_docs, key_docs, grads_out, attended, row_max, row_sum = (
        operands
    )
    scaling = queries.shape[1] ** (-0.5)
    slot_span = queries.shape[0]
    deltas = jnp.sum(grads_out.astype(jnp.float32) * attended.astype(jnp.float32), axis=1)
    visible = visible_pairs(query_docs, key_docs)
    weights_low, score_grads = weight_terms(
        queries, key_rows, value_rows, visible, row_max, row_sum, grads_out, deltas
    )
    query_grads = jnp.dot(score_grads, key_rows, preferred_element_type=jnp.float32) * scaling
    key_grads = jnp.dot(score_grads.T, queries, preferred_element_type=jnp.float32) * scaling
    value_grads = jnp.dot(weights_low.T, grads_out, preferred_element_type=jnp.float32)
    return (query_grads, key_grads, value_grads, deltas)


def fill_slots(flat_rows, source, filled, slot_shape):
    taken = jnp.take(flat_rows, source, axis=0)
    kept = jnp.where(filled[:, None], taken, jnp.zeros_like(taken))
    return kept.reshape(slot_shape)


def per_device(projections, routed_heads, slot_index, gate_logits, doc_lengths, cotangent):
    token_count = projections.shape[0]
    route_count = routed_heads.shape[1]
    full_width = projections.shape[2]
    head_size = full_width // 3
    head_groups = lax.axis_size("head")
    offset = (lax.axis_index("seq") * head_groups + lax.axis_index("head")) * token_count
    positions = offset + jnp.arange(token_count, dtype=jnp.int32)
    doc_ends = jnp.cumsum(doc_lengths)
    documents = jnp.sum((positions[:, None] >= doc_ends[None, :]).astype(jnp.int32), axis=1) + 1
    gate_values = jax.nn.sigmoid(gate_logits)
    grads_out = (cotangent.astype(jnp.float32) * gate_values[:, :, None]).astype(jnp.bfloat16)
    flat_dest = (routed_heads * CAP + slot_index).reshape(token_count * route_count)
    route_ids = jnp.arange(token_count * route_count, dtype=jnp.int32)
    source_raw = jnp.full((H * CAP,), -1, jnp.int32).at[flat_dest].set(route_ids)
    filled = source_raw >= 0
    source = jnp.maximum(source_raw, 0)
    proj_slots = fill_slots(
        projections.reshape(token_count * route_count, full_width),
        source,
        filled,
        (H, CAP, full_width),
    )
    out_slots = fill_slots(
        grads_out.reshape(token_count * route_count, head_size), source, filled, (H, CAP, head_size)
    )
    doc_slots = jnp.where(filled, jnp.take(documents, source // route_count, axis=0), 0).reshape(
        H, CAP
    )
    owned_rows, owned_docs = (
        lax.all_to_all(proj_slots, "head", split_axis=0, concat_axis=1, tiled=True),
        lax.all_to_all(doc_slots, "head", split_axis=0, concat_axis=1, tiled=True),
    )
    earlier_rows, earlier_docs = shifted((owned_rows[:, :, head_size:], owned_docs), "seq", 1)
    slot_span = owned_docs.shape[1]
    queries = owned_rows[:, :, :head_size]
    key_rows = jnp.concatenate(
        [earlier_rows[:, :, :head_size], owned_rows[:, :, head_size : 2 * head_size]], 1
    )
    value_rows = jnp.concatenate(
        [earlier_rows[:, :, head_size:], owned_rows[:, :, 2 * head_size :]], 1
    )
    key_docs = jnp.concatenate([earlier_docs, owned_docs], 1)
    attended, row_max, row_sum = lax.map(
        forward_head, (queries, key_rows, value_rows, owned_docs, key_docs)
    )
    returned = lax.all_to_all(attended, "head", split_axis=1, concat_axis=0, tiled=True)
    returned_flat = returned.reshape(H * CAP, head_size)
    owned_out = lax.all_to_all(out_slots, "head", split_axis=0, concat_axis=1, tiled=True)
    backward_operands = (
        queries,
        key_rows,
        value_rows,
        owned_docs,
        key_docs,
        owned_out,
        attended,
        row_max,
        row_sum,
    )
    query_grads, key_grads, value_grads, deltas = lax.map(
        partial(backward_head, keep_earlier=True), backward_operands
    )
    incoming = shifted(
        jnp.concatenate([key_grads[:, :slot_span], value_grads[:, :slot_span]], 2).astype(
            jnp.bfloat16
        ),
        "seq",
        -1,
    ).astype(jnp.float32)
    own_keys = key_grads[:, slot_span:] + incoming[:, :, :head_size]
    own_values = value_grads[:, slot_span:] + incoming[:, :, head_size:]
    gradients = jnp.concatenate([query_grads, own_keys, own_values], 2).astype(jnp.bfloat16)
    grads_home = lax.all_to_all(gradients, "head", split_axis=1, concat_axis=0, tiled=True)
    token_attended = jnp.take(returned_flat, flat_dest, axis=0).reshape(
        token_count, route_count, head_size
    )
    projection_grads = jnp.take(grads_home.reshape(H * CAP, full_width), flat_dest, axis=0).reshape(
        token_count, route_count, full_width
    )
    attended_wide = token_attended.astype(jnp.float32)
    head_outputs = (attended_wide * gate_values[:, :, None]).astype(jnp.bfloat16)
    gate_grads = (
        jnp.sum(cotangent.astype(jnp.float32) * attended_wide, axis=2)
        * gate_values
        * (1.0 - gate_values)
    )
    return (head_outputs, projection_grads, gate_grads)


def solution(mesh):
    return jax.shard_map(
        per_device,
        mesh=mesh,
        in_specs=(
            P(("seq", "head"), None, None),
            P(("seq", "head"), None),
            P(("seq", "head"), None),
            P(("seq", "head"), None),
            P(),
            P(("seq", "head"), None, None),
        ),
        out_specs=(
            P(("seq", "head"), None, None),
            P(("seq", "head"), None, None),
            P(("seq", "head"), None),
        ),
        check_vma=False,
    )
```

profile of v0, /device:TPU:9, one launch (start us, length us, event | category | flops | bytes accessed | tf_op | source)
XLA Modules:
  0.0 720.2 jit_solution(14332878141005288111)
XLA Ops:
  10.9 19.4 %gather_fusion = s32[3072]{0:T(1024)S(1)} fusion(s32[192]{0:T(256)S(1)} %broadcast_add_fusion, s32[3072]{0:T(1024)S(1)} %broadcast_clamp_fusion), kind=kCustom, calls=%fused_computation | custom fusion | bytes 36864 | tf_op jit(solution)/shard_map/jit(_take)/gather | solution.py:106
  31.0 11.0 %gather_fusion.1 = bf16[3072,384]{1,0:T(8,128)(2,1)S(1)} fusion(bf16[1536,384]{1,0:T(8,128)(2,1)S(1)} %bitcast.134, s32[3072]{0:T(1024)S(1)} %get-tuple-element.355), kind=kCustom, calls=%fused_computation.1 | custom fusion | bytes 4730880 | tf_op jit(solution)/shard_map/jit(_take)/gather | solution.py:75
  44.3 30.2 %all_to_all.85 = bf16[64,48,384]{2,1,0:T(8,128)(2,1)S(1)} all-to-all(bf16[64,48,384]{2,1,0:T(8,128)(2,1)S(1)} %select_select_fusion), channel_id=1, replica_groups=mesh['seq'=8,'head'=4] {'head'}, dimensions={0} | all-to-all | bytes 4718592 | tf_op jit(solution)/shard_map/all_to_all | solution.py:110
  83.5 6.8 all_to_all.86
  105.5 116.0 %while.32 = (s32[]{:T(128)}, bf16[16,192,128]{2,1,0:T(8,128)(2,1)S(1)}, f32[16,192]{1,0:T(8,128)}, f32[16,192]{1,0:T(8,128)}, s32[16,384]{1,0:T(8,128)}, /*index...) while((s32[]{:T(128)}, ...), condition=%wide.region_6.7_spmd, body=%wide.region_3.6_spmd.sunk | while | flops 38658432 | bytes 1305033 | solution.py:123
  243.7 10.7 %gather_fusion.3 = bf16[3072,128]{1,0:T(8,128)(2,1)S(1)} fusion(bf16[1536,128]{1,0:T(8,128)(2,1)S(1)} %get-tuple-element.352, s32[3072]{0:T(1024)} %copy-done.9), kind=kCustom, calls=%fused_computation.3 | custom fusion | bytes 1585152 | tf_op jit(solution)/shard_map/jit(_take)/gather | solution.py:75
  260.2 10.2 %all-to-all-done.3 = bf16[64,48,128]{2,1,0:T(8,128)(2,1)S(1)} async-done(((bf16[64,48,128]{2,1,0:T(8,128)(2,1)}), bf16[64,48,128]{2,1,0:T(8,128)(2,1)S(1)}, u32[]{:S(2)}, u32[]{:S(2)}) %all-to-all-start.3) | async-done | bytes 786464 | tf_op jit(solution)/shard_map/all_to_all | solution.py:128
  270.5 377.7 %while.33 = (s32[]{:T(128)}, bf16[16,192,128]{2,0,1:T(8,128)(2,1)}, f32[16,384,128]{2,0,1:T(8,128)}, f32[16,384,128]{2,0,1:T(8,128)}, s32[16,384]{1,0:T(8,128)},...) while((s32[]{:T(128)}, bf16[16,192,128]{2,0,1:T(8,128)(2,1)}, ...), condition=%wide.region_9.10_spmd, body=%wide.region_7.9_spmd.sunk | while | flops 95429184 | bytes 3412417 | solution.py:140
  287.7 6.4 dynamic_update_slice.52
  311.3 6.4 dynamic_update_slice.52
  334.9 6.4 dynamic_update_slice.52
  382.0 6.4 dynamic_update_slice.52
  429.2 6.4 dynamic_update_slice.52
  452.8 6.4 dynamic_update_slice.52
  476.4 6.4 dynamic_update_slice.52
  500.0 6.4 dynamic_update_slice.52
  523.6 6.4 dynamic_update_slice.52
  547.3 6.4 dynamic_update_slice.52
  570.9 6.4 dynamic_update_slice.52
  594.5 6.4 dynamic_update_slice.52
  618.1 6.4 dynamic_update_slice.52
  641.7 6.4 dynamic_update_slice.52
  655.1 19.4 %collective-permute-done.2 = bf16[16,192,256]{2,0,1:T(8,128)(2,1)S(1)} collective-permute-done((bf16[16,192,256]{2,0,1:T(8,128)(2,1)S(1)}, bf16[16,192,256]{2,0,1:T(8,128)(2,1)S(1)}, u32[]{:S(2)}, u32[]{:S(2)}) %collective-permute-start.2) | collective-permute-done | bytes 1572896 | tf_op jit(solution)/shard_map/ppermute | solution.py:18
  684.6 24.1 %all-to-all-done.4 = bf16[16,192,384]{2,0,1:T(8,128)(2,1)S(1)} async-done(((bf16[16,192,384]{2,0,1:T(8,128)(2,1)}), bf16[16,192,384]{2,0,1:T(8,128)(2,1)S(1)}, u32[]{:S(2)}, u32[]{:S(2)}) %all-to-all-start.4) | async-done | bytes 2359328 | tf_op jit(solution)/shard_map/all_to_all | solution.py:153
  (531 shorter events, 496.5 us)
Async XLA Ops:
  0.6 30.3 %copy-start = (bf16[192,8,384]{2,1,0:T(8,128)(2,1)S(1)}, bf16[192,8,384]{2,1,0:T(8,128)(2,1)}, u32[]{:S(2)}) copy-start(bf16[192,8,384]{2,1,0:T(8,128)(2,1)} %param.10) | copy-start | bytes 3538948
  2.3 6.2 copy-start.16
  31.0 11.0 %copy-start.9 = (s32[3072]{0:T(1024)}, s32[3072]{0:T(1024)S(1)}, u32[]{:S(2)}) copy-start(s32[3072]{0:T(1024)S(1)} %get-tuple-element.355) | copy-start | bytes 36868
  74.8 6.6 copy-start.15
  76.1 26.5 %collective-permute-start.1 = (bf16[16,192,256]{2,1,0:T(8,128)(2,1)}, bf16[16,192,256]{2,1,0:T(8,128)(2,1)}, u32[]{:S(2)}, u32[]{:S(2)}) collective-permute-start(bf16[16,192,256]{2,1,0:T(8,128)(2,1)} %slice.61), channel_id=1, source_target_pairs={{0,4},{4,8},{8,12},{12,16},{16,20},{20,24},{24,28},{1,5},{5,9},{9,... | collective-permute-start | bytes 4718600 | tf_op jit(solution)/shard_map/ppermute | solution.py:18
  95.7 3.9 collective-permute-start
  104.1 1.4 copy-start.5
  108.2 1.1 copy-start.10
  115.5 1.1 copy-start.10
  130.0 1.1 copy-start.10
  221.5 1.4 copy-start.2
  222.9 13.7 %all-to-all-start.2 = ((bf16[16,192,128]{2,0,1:T(8,128)(2,1)}), bf16[16,192,128]{2,0,1:T(8,128)(2,1)S(1)}, u32[]{:S(2)}, u32[]{:S(2)}) async-start(bf16[16,192,128]{2,0,1:T(8,128)(2,1)} %copy.58), calls=%async_computation.2 | async-start | bytes 1572864 | tf_op jit(solution)/shard_map/all_to_all | solution.py:126
  228.5 8.1 %copy-start.6 = (f32[192,8]{1,0:T(8,128)}, f32[192,8]{1,0:T(8,128)S(1)}, u32[]{:S(2)}) copy-start(f32[192,8]{1,0:T(8,128)S(1)} %copy.60) | copy-start | bytes 18436
  236.8 3.8 copy-start.8
  243.6 10.8 %copy-start.12 = (pred[64,48]{1,0:T(8,128)(4,1)S(1)}, pred[64,48]{1,0:T(8,128)(4,1)}, u32[]{:S(2)}) copy-start(pred[64,48]{1,0:T(8,128)(4,1)} %broadcast_in_dim.167) | copy-start | bytes 9220
  243.7 10.8 %copy-start.13 = (pred[64,48]{1,0:T(8,128)(4,1)S(1)}, pred[64,48]{1,0:T(8,128)(4,1)}, u32[]{:S(2)}) copy-start(pred[64,48]{1,0:T(8,128)(4,1)} %broadcast_in_dim.169) | copy-start | bytes 9220
  256.6 13.7 %all-to-all-start.3 = ((bf16[64,48,128]{2,1,0:T(8,128)(2,1)}), bf16[64,48,128]{2,1,0:T(8,128)(2,1)S(1)}, u32[]{:S(2)}, u32[]{:S(2)}) async-start(bf16[64,48,128]{2,1,0:T(8,128)(2,1)} %select_select_fusion.1), calls=%async_computation.3 | async-start | bytes 1572864 | tf_op jit(solution)/shard_map/all_to_all | solution.py:128
  651.2 23.7 %copy-start.4 = (f32[16,384,128]{2,0,1:T(8,128)S(1)}, f32[16,384,128]{2,0,1:T(8,128)}, u32[]{:S(2)}) copy-start(f32[16,384,128]{2,0,1:T(8,128)} %get-tuple-element.285) | copy-start | bytes 9437188
  651.4 23.5 %copy-start.3 = (f32[16,384,128]{2,0,1:T(8,128)S(1)}, f32[16,384,128]{2,0,1:T(8,128)}, u32[]{:S(2)}) copy-start(f32[16,384,128]{2,0,1:T(8,128)} %get-tuple-element.286) | copy-start | bytes 9437188
  651.4 23.1 %collective-permute-start.2 = (bf16[16,192,256]{2,0,1:T(8,128)(2,1)S(1)}, bf16[16,192,256]{2,0,1:T(8,128)(2,1)S(1)}, u32[]{:S(2)}, u32[]{:S(2)}) collective-permute-start(bf16[16,192,256]{2,0,1:T(8,128)(2,1)S(1)} %pad_maximum_fusion.3), channel_id=1, source_target_pairs={{4,0},{8,4},{12,8},{16,12},{20,16},{24,20},{28,24},{5,1},{9,5},{13... | collective-permute-start | bytes 4718600 | tf_op jit(solution)/shard_map/ppermute | solution.py:18
  674.9 1.1 copy-start.7
  677.8 31.0 %all-to-all-start.4 = ((bf16[16,192,384]{2,0,1:T(8,128)(2,1)}), bf16[16,192,384]{2,0,1:T(8,128)(2,1)S(1)}, u32[]{:S(2)}, u32[]{:S(2)}) async-start(bf16[16,192,384]{2,0,1:T(8,128)(2,1)} %pad_maximum_fusion), calls=%async_computation.4 | async-start | bytes 4718592 | tf_op jit(solution)/shard_map/all_to_all | solution.py:153
  708.7 1.4 copy-start.1
  710.1 2.2 copy-start.14
  (29 other events, 28.9 us)
where the time goes:
time: 735 us; the launch traced here: 720 us
  local copies, waits for them, and re-layouts  438 us (60%)
  matrix products  108 us (15%)
  waiting for transfers between devices  60.7 us (8%)
  other arithmetic  51.3 us (7%)
  blocking collectives  36.9 us (5%)
  starting transfers between devices  22.7 us (3%)
    dynamic_update_slice x48, local copies, waits for them, and re-layouts, per_device(): lax.map(partial(backward_head, keep_earlier=True), backward_operands)  265 us
    dynamic_update_slice x48, local copies, waits for them, and re-layouts, per_device(): lax.map(forward_head, (queries, key_rows, value_rows, owned_docs, key_docs))  54.6 us
    dot_general x32, matrix products, masked_scores(): jnp.dot(queries, key_rows.T, preferred_element_type=jnp.float32) * scaling  38.2 us
    all_to_all x1, blocking collectives, per_device(): lax.all_to_all(proj_slots, 'head', split_axis=0, concat_axis=1, tiled=True)  30.2 us
    all_to_all x1, waiting for transfers between devices, per_device(): lax.all_to_all(gradients, 'head', split_axis=1, concat_axis=0, tiled=True)  24.1 us
    dynamic_slice x64, local copies, waits for them, and re-layouts, per_device(): lax.map(forward_head, (queries, key_rows, value_rows, owned_docs, key_docs))  23.7 us
    gt x32, other arithmetic, visible_pairs(): key_docs[None, :] > 0  23.3 us
    gather x2, local copies, waits for them, and re-layouts, fill_slots(): taken = jnp.take(flat_rows, source, axis=0)  21.7 us
  transfers between devices with their start and end apart: 6, of which 5 were waited for; matrix products, arithmetic and copies ran while one was open for 2% of the time, Pallas kernels for 0%

commit v1 on v0

v1 whole, which is shorter than its diff:
```python
from functools import partial

import jax
import jax.numpy as jnp
from jax import lax
from jax.experimental import pallas as pl
from jax.experimental.pallas import tpu as pltpu
from jax.sharding import PartitionSpec as P

H = 64
CAP = 48
MASKED = -1e30
DOC_ROWS = 16
DOC_LANES = 64
PARTS = (6, 6, 4)
VMEM_LIMIT = 56 * 1024 * 1024

VMEM = pl.BlockSpec(memory_space=pltpu.VMEM)


def head_chunks(heads):
    total = sum(PARTS)
    edges = [0]
    for i in range(len(PARTS)):
        edges.append(round(heads * sum(PARTS[: i + 1]) / total))
    return [(a, b - a) for a, b in zip(edges[:-1], edges[1:]) if b > a]


def call(kernel, out_shape, *operands, aliases=None):
    return pl.pallas_call(
        kernel,
        out_shape=out_shape,
        in_specs=[VMEM] * len(operands),
        out_specs=jax.tree.map(lambda _: VMEM, out_shape),
        input_output_aliases=aliases or {},
        compiler_params=pltpu.CompilerParams(vmem_limit_bytes=VMEM_LIMIT),
    )(*operands)


def dot(a, b, dims):
    return lax.dot_general(a, b, (dims, ((), ())), preferred_element_type=jnp.float32)


NN = ((1,), (0,))
NT = ((1,), (1,))
TN = ((0,), (0,))


def dispatch_kernel(first, count, owned, flat_ref, doc_ref, proj_ref, out_grad_ref, *out_refs):
    me = lax.axis_index("head")
    rows = count * CAP
    routes = flat_ref.shape[1]
    width = proj_ref.shape[1]
    head_size = out_grad_ref.shape[1]
    flat = flat_ref[...]
    docs = doc_ref[...]
    lane = lax.broadcasted_iota(jnp.int32, (CAP, DOC_LANES), 1)
    for d, out_ref in enumerate(out_refs):
        base = ((me ^ d) * owned + first) * CAP
        hit = lax.broadcasted_iota(jnp.int32, (rows, routes), 0) == flat - base
        one_hot = jnp.where(hit, 1.0, 0.0).astype(jnp.bfloat16)
        out_ref[:rows, :width] = dot(one_hot, proj_ref[...], NN).astype(jnp.bfloat16)
        out_ref[:rows, width:] = dot(one_hot, out_grad_ref[...], NN).astype(jnp.bfloat16)
        slot_docs = jnp.sum(jnp.where(hit, docs, 0.0), axis=1, keepdims=True)
        table = jnp.zeros((CAP, DOC_LANES), jnp.float32)
        for h in range(count):
            table = jnp.where(lane == h, slot_docs[h * CAP : (h + 1) * CAP], table)
        thirds = [table[i * DOC_ROWS : (i + 1) * DOC_ROWS] for i in range(CAP // DOC_ROWS)]
        packed = jnp.concatenate(thirds + [jnp.zeros_like(thirds[0])], 1)
        blank = jnp.zeros((DOC_ROWS, head_size), jnp.float32)
        out_ref[rows:, :] = jnp.concatenate([blank, packed, blank], 1).astype(jnp.bfloat16)


def doc_table(packed):
    packed = packed.astype(jnp.float32)
    thirds = [packed[:, i * DOC_LANES : (i + 1) * DOC_LANES] for i in range(CAP // DOC_ROWS)]
    return jnp.concatenate(thirds, 0)


def attention_kernel(count, groups, *refs):
    blocks = refs[:groups]
    before_ref = refs[groups]
    near_ref, far_ref, own_ref, mask_ref = refs[groups + 1 :]
    me = lax.axis_index("head")
    rows = count * CAP
    head_size = blocks[0].shape[1] // 4
    scaling = head_size ** (-0.5)
    span = groups * CAP
    query_docs = jnp.concatenate(
        [doc_table(b[rows:, head_size : 3 * head_size]) for b in blocks], 0
    )
    before_docs = jnp.concatenate([doc_table(before_ref[d, rows:, :]) for d in range(groups)], 0)
    key_docs = jnp.concatenate([before_docs, query_docs], 0)
    key_docs = jnp.concatenate([key_docs, jnp.zeros_like(key_docs)], 1).T

    def order(index):
        return (me ^ (index // CAP)) * CAP + index % CAP

    row_order = order(lax.broadcasted_iota(jnp.int32, (span, 1), 0))
    column = lax.broadcasted_iota(jnp.int32, (1, 2 * span), 1)
    column_order = jnp.where(column < span, -1, order(jnp.maximum(column - span, 0)))
    mask_ref[...] = jnp.where(column_order <= row_order, 0.0, MASKED)

    for h in range(count):
        here = slice(h * CAP, (h + 1) * CAP)

        def piece(i):
            return jnp.concatenate([b[here, i * head_size : (i + 1) * head_size] for b in blocks], 0)

        def before(i):
            return jnp.concatenate(
                [before_ref[d, here, i * head_size : (i + 1) * head_size] for d in range(groups)], 0
            )

        queries = piece(0)
        key_rows = jnp.concatenate([before(0), piece(1)], 0)
        value_rows = jnp.concatenate([before(1), piece(2)], 0)
        grads_out = piece(3)
        scores = dot(queries, key_rows, NT) * scaling + mask_ref[...]
        scores = jnp.where(key_docs[h : h + 1, :] == query_docs[:, h : h + 1], scores, MASKED)
        row_max = jnp.max(scores, axis=1, keepdims=True)
        powers = jnp.exp(scores - row_max)
        row_sum = jnp.sum(powers, axis=1, keepdims=True)
        weights = powers * (1.0 / row_sum)
        weights_low = weights.astype(jnp.bfloat16)
        attended = dot(weights_low, value_rows, NN).astype(jnp.bfloat16)
        deltas = jnp.sum(
            grads_out.astype(jnp.float32) * attended.astype(jnp.float32), axis=1, keepdims=True
        )
        weight_grads = dot(grads_out, value_rows, NT)
        score_grads = (weights * (weight_grads - deltas)).astype(jnp.bfloat16)
        query_grads = (dot(score_grads, key_rows, NN) * scaling).astype(jnp.bfloat16)
        key_grads = dot(score_grads, queries, TN) * scaling
        value_grads = dot(weights_low, grads_out, TN)
        for d in range(groups):
            part = slice(d * CAP, (d + 1) * CAP)
            own = slice(span + d * CAP, span + (d + 1) * CAP)
            near_ref[d, here, :head_size] = attended[part]
            near_ref[d, here, head_size:] = query_grads[part]
            far_ref[d, here, :head_size] = key_grads[part].astype(jnp.bfloat16)
            far_ref[d, here, head_size:] = value_grads[part].astype(jnp.bfloat16)
            own_ref[d, here, :head_size] = key_grads[own]
            own_ref[d, here, head_size:] = value_grads[own]


def combine_kernel(groups, near_ref, own_ref, incoming_ref, *out_refs):
    half = near_ref.shape[2]
    for d in range(groups):
        out_refs[d][:, :half] = near_ref[d]
        total = own_ref[d] + incoming_ref[d].astype(jnp.float32)
        out_refs[d][:, half:] = total.astype(jnp.bfloat16)


def return_kernel(first, count, owned, groups, initial, *refs):
    flat_ref = refs[0]
    blocks = refs[1 : groups + 1]
    total_ref = None if initial else refs[groups + 1]
    out_ref = refs[-1]
    me = lax.axis_index("head")
    rows = count * CAP
    routes, lanes = flat_ref.shape
    tile = 256
    all_rows = jnp.concatenate([b[...] for b in blocks], 0)
    column = lax.broadcasted_iota(jnp.int32, (1, groups * rows), 1)
    slot = ((me ^ (column // rows)) * owned + first) * CAP + column % rows
    for start in range(0, routes, tile):
        part = slice(start, start + tile)
        hit = flat_ref[part, 0:1] == slot
        one_hot = jnp.where(hit, 1.0, 0.0).astype(jnp.bfloat16)
        taken = dot(one_hot, all_rows, NN)
        if not initial:
            taken = taken + total_ref[part, :].astype(jnp.float32)
        out_ref[part, :] = taken.astype(jnp.bfloat16)


def shifted(block, axis, distance):
    devices = range(lax.axis_size(axis))
    route = [(i, i + distance) for i in devices if i + distance in devices]
    return lax.ppermute(block, axis, route)


def exchanged(blocks):
    groups = len(blocks)
    return [blocks[0]] + [
        lax.ppermute(blocks[d], "head", [(i, i ^ d) for i in range(groups)])
        for d in range(1, groups)
    ]


def per_device(projections, routed_heads, slot_index, gate_logits, doc_lengths, cotangent):
    tokens, top, width = projections.shape
    head_size = width // 3
    routes = tokens * top
    groups = lax.axis_size("head")
    owned = H // groups
    bf16, f32 = jnp.bfloat16, jnp.float32

    offset = (lax.axis_index("seq") * groups + lax.axis_index("head")) * tokens
    positions = offset + jnp.arange(routes, dtype=jnp.int32) // top
    doc_ends = jnp.cumsum(doc_lengths)
    documents = jnp.sum((positions[None, :] >= doc_ends[:, None]).astype(f32), axis=0) + 1.0
    gate_values = jax.nn.sigmoid(gate_logits)
    grads_out = (cotangent.astype(f32) * gate_values[:, :, None]).astype(bf16)
    flat = (routed_heads * CAP + slot_index).reshape(routes)
    flat_columns = jnp.broadcast_to(flat[:, None], (routes, 128))
    rows_in = projections.reshape(routes, width)
    grads_in = grads_out.reshape(routes, head_size)

    chunks = head_chunks(owned)
    received = []
    for first, count in chunks:
        rows = count * CAP
        sent = call(
            partial(dispatch_kernel, first, count, owned),
            [jax.ShapeDtypeStruct((rows + DOC_ROWS, width + head_size), bf16)] * groups,
            flat[None, :],
            documents[None, :],
            rows_in,
            grads_in,
        )
        received.append(exchanged(sent))

    totals = None
    for (first, count), blocks in zip(chunks, received):
        rows = count * CAP
        before = shifted(jnp.stack([b[:, head_size : 3 * head_size] for b in blocks]), "seq", 1)
        pair = (groups, rows, 2 * head_size)
        near, far, own = pl.pallas_call(
            partial(attention_kernel, count, groups),
            out_shape=[
                jax.ShapeDtypeStruct(pair, bf16),
                jax.ShapeDtypeStruct(pair, bf16),
                jax.ShapeDtypeStruct(pair, f32),
            ],
            in_specs=[VMEM] * (groups + 1),
            out_specs=[VMEM] * 3,
            scratch_shapes=[pltpu.VMEM((groups * CAP, 2 * groups * CAP), f32)],
            compiler_params=pltpu.CompilerParams(vmem_limit_bytes=VMEM_LIMIT),
        )(*blocks, before)
        incoming = shifted(far, "seq", -1)
        home = call(
            partial(combine_kernel, groups),
            [jax.ShapeDtypeStruct((rows, 4 * head_size), bf16)] * groups,
            near,
            own,
            incoming,
        )
        home = exchanged(home)
        more = [] if totals is None else [totals]
        totals = call(
            partial(return_kernel, first, count, owned, groups, totals is None),
            jax.ShapeDtypeStruct((routes, 4 * head_size), bf16),
            flat_columns,
            *home,
            *more,
            aliases={groups + 1: 0} if more else None,
        )

    attended = totals[:, :head_size].reshape(tokens, top, head_size).astype(f32)
    projection_grads = totals[:, head_size:].reshape(tokens, top, width)
    head_outputs = (attended * gate_values[:, :, None]).astype(bf16)
    gate_grads = (
        jnp.sum(cotangent.astype(f32) * attended, axis=2) * gate_values * (1.0 - gate_values)
    )
    return (head_outputs, projection_grads, gate_grads)


def solution(mesh):
    return jax.shard_map(
        per_device,
        mesh=mesh,
        in_specs=(
            P(("seq", "head"), None, None),
            P(("seq", "head"), None),
            P(("seq", "head"), None),
            P(("seq", "head"), None),
            P(),
            P(("seq", "head"), None, None),
        ),
        out_specs=(
            P(("seq", "head"), None, None),
            P(("seq", "head"), None, None),
            P(("seq", "head"), None),
        ),
        check_vma=False,
    )
```

time: 735 us -> 161 us (0.22)
  the two profiles are of different devices: /device:TPU:9 before, /device:TPU:16 now
where the time goes in v1:
time: 161 us; the launch traced here: 160 us
  Pallas kernels  57.8 us (36%)
  waiting for transfers between devices  43.2 us (27%)
  starting transfers between devices  38.3 us (24%)
  local copies, waits for them, and re-layouts  14.1 us (9%)
  other arithmetic  5.35 us (3%)
    ppermute x18, waiting for transfers between devices, exchanged(): lax.ppermute(blocks[d], 'head', [(i, i ^ d) for i in range(groups)])  37.6 us
    pallas_call x9, Pallas kernels, call(): pl.pallas_call(kernel, out_shape=out_shape, in_specs=[VMEM] * len(operand...  37 us
    ppermute x18, starting transfers between devices, exchanged(): lax.ppermute(blocks[d], 'head', [(i, i ^ d) for i in range(groups)])  23 us
    pallas_call x3, Pallas kernels, per_device(): pl.pallas_call(partial(attention_kernel, count, groups), out_shape=[jax.S...  20.8 us
    ppermute x6, starting transfers between devices, shifted(): return lax.ppermute(block, axis, route)  15.3 us
    unnamed x64, local copies, waits for them, and re-layouts  7.18 us
    ppermute x6, waiting for transfers between devices, shifted(): return lax.ppermute(block, axis, route)  5.56 us
  transfers between devices with their start and end apart: 24, of which 9 were waited for; matrix products, arithmetic and copies ran while one was open for 2% of the time, Pallas kernels for 31%

profile of v1, /device:TPU:16, one launch (start us, length us, event | category | flops | bytes accessed | tf_op | source)
XLA Modules:
  0.0 159.7 jit_solution(11281060903327137558)
XLA Ops:
  6.6 4.3 %shard_map.85 = (bf16[208,512]{1,0:T(8,128)(2,1)}, bf16[208,512]{1,0:T(8,128)(2,1)}, bf16[208,512]{1,0:T(8,128)(2,1)}, bf16[208,512]{1,0:T(8,128)(2,1)}) custom-call(s32[1,1536]{1,0:T(1,128)} %broadcast_in_dim_reshape.2.flat_ref, f32[1,1536]{1,0:T(1,128)} %add.46.doc_ref, bf16[1536,384]{1,0:T(8,128)(2,1)} %bitcast.37, bf16[1536,128]{1,0:T(8,128)(2,1)} %fusion.3.out_grad_ref), custom_call_target="tpu_custom_call" | custom-call | tf_op jit(solution)/shard_map/pallas_call | solution.py:30
  14.4 5.1 %shard_map.88 = (bf16[304,512]{1,0:T(8,128)(2,1)}, bf16[304,512]{1,0:T(8,128)(2,1)}, bf16[304,512]{1,0:T(8,128)(2,1)}, bf16[304,512]{1,0:T(8,128)(2,1)}) custom-call(s32[1,1536]{1,0:T(1,128)} %broadcast_in_dim_reshape.2.flat_ref, f32[1,1536]{1,0:T(1,128)} %add.46.doc_ref, bf16[1536,384]{1,0:T(8,128)(2,1)} %bitcast.38, bf16[1536,128]{1,0:T(8,128)(2,1)} %fusion.3.out_grad_ref), custom_call_target="tpu_custom_call" | custom-call | tf_op jit(solution)/shard_map/pallas_call | solution.py:30
  22.4 5.1 %shard_map.91 = (bf16[304,512]{1,0:T(8,128)(2,1)}, bf16[304,512]{1,0:T(8,128)(2,1)}, bf16[304,512]{1,0:T(8,128)(2,1)}, bf16[304,512]{1,0:T(8,128)(2,1)}) custom-call(s32[1,1536]{1,0:T(1,128)} %broadcast_in_dim_reshape.2.flat_ref, f32[1,1536]{1,0:T(1,128)} %add.46.doc_ref, bf16[1536,384]{1,0:T(8,128)(2,1)} %bitcast.39, bf16[1536,128]{1,0:T(8,128)(2,1)} %fusion.3.out_grad_ref), custom_call_target="tpu_custom_call" | custom-call | tf_op jit(solution)/shard_map/pallas_call | solution.py:30
  31.9 5.3 %collective-permute-done.9.refs_2_ = bf16[304,512]{1,0:T(8,128)(2,1)S(1)} collective-permute-done((bf16[304,512]{1,0:T(8,128)(2,1)}, bf16[304,512]{1,0:T(8,128)(2,1)S(1)}, u32[]{:S(2)}, u32[]{:S(2)}) %collective-permute-start.9) | collective-permute-done | bytes 311328 | tf_op jit(solution)/shard_map/ppermute | solution.py:185
  40.3 8.2 %collective-permute-done.18.refs_3_ = bf16[304,512]{1,0:T(8,128)(2,1)S(1)} collective-permute-done((bf16[304,512]{1,0:T(8,128)(2,1)}, bf16[304,512]{1,0:T(8,128)(2,1)S(1)}, u32[]{:S(2)}, u32[]{:S(2)}) %collective-permute-start.18) | collective-permute-done | bytes 311328 | tf_op jit(solution)/shard_map/ppermute | solution.py:185
  50.3 5.8 %collective-permute-done.17.refs_2_ = bf16[304,512]{1,0:T(8,128)(2,1)S(1)} collective-permute-done((bf16[304,512]{1,0:T(8,128)(2,1)S(1)}, bf16[304,512]{1,0:T(8,128)(2,1)S(1)}, u32[]{:S(2)}, u32[]{:S(2)}) %collective-permute-start.17) | collective-permute-done | bytes 311328 | tf_op jit(solution)/shard_map/ppermute | solution.py:185
  58.2 3.8 %collective-permute-start.19 = (bf16[4,304,256]{2,1,0:T(8,128)(2,1)S(1)}, bf16[4,304,256]{2,1,0:T(8,128)(2,1)S(1)}, u32[]{:S(2)}, u32[]{:S(2)}) collective-permute-start(bf16[4,304,256]{2,1,0:T(8,128)(2,1)S(1)} %pad_maximum_fusion.1), channel_id=1, source_target_pairs={{0,4},{4,8},{8,12},{12,16},{16,20},{20,24},{24,28},{1,5},{5,9},{9,... | collective-permute-start | bytes 1867784 | tf_op jit(solution)/shard_map/ppermute | solution.py:179
  62.1 5.5 %collective-permute-done.11.refs_4_ = bf16[4,304,256]{2,1,0:T(8,128)(2,1)S(1)} collective-permute-done((bf16[4,304,256]{2,1,0:T(8,128)(2,1)S(1)}, bf16[4,304,256]{2,1,0:T(8,128)(2,1)S(1)}, u32[]{:S(2)}, u32[]{:S(2)}) %collective-permute-start.11) | collective-permute-done | bytes 622624 | tf_op jit(solution)/shard_map/ppermute | solution.py:179
  68.5 7.5 %shard_map.89 = (bf16[4,288,256]{2,1,0:T(8,128)(2,1)}, bf16[4,288,256]{2,1,0:T(8,128)(2,1)}, f32[4,288,256]{2,1,0:T(8,128)}) custom-call(bf16[304,512]{1,0:T(8,128)(2,1)} %get-tuple-element.47.refs_0_, bf16[304,512]{1,0:T(8,128)(2,1)} %copy-done.6, bf16[304,512]{1,0:T(8,128)(2,1)} %copy-done.2, bf16[304,512]{1,0:T(8,128)(2,1)} %copy-done.3, ...), custom_call_target="tpu_custom_call" | custom-call | tf_op jit(solution)/shard_map/pallas_call | solution.py:228
  78.0 2.4 %collective-permute-start.3 = (bf16[4,208,256]{2,1,0:T(8,128)(2,1)S(1)}, bf16[4,208,256]{2,1,0:T(8,128)(2,1)S(1)}, u32[]{:S(2)}, u32[]{:S(2)}) collective-permute-start(bf16[4,208,256]{2,1,0:T(8,128)(2,1)S(1)} %pad_maximum_fusion.2), channel_id=1, source_target_pairs={{0,4},{4,8},{8,12},{12,16},{16,20},{20,24},{24,28},{1,5},{5,9},{9,... | collective-permute-start | bytes 1277960 | tf_op jit(solution)/shard_map/ppermute | solution.py:179
  81.3 7.6 %shard_map.92 = (bf16[4,288,256]{2,1,0:T(8,128)(2,1)}, bf16[4,288,256]{2,1,0:T(8,128)(2,1)}, f32[4,288,256]{2,1,0:T(8,128)}) custom-call(bf16[304,512]{1,0:T(8,128)(2,1)} %get-tuple-element.58.refs_0_, bf16[304,512]{1,0:T(8,128)(2,1)} %copy-done.5, bf16[304,512]{1,0:T(8,128)(2,1)} %copy-done.7, bf16[304,512]{1,0:T(8,128)(2,1)} %copy-done.4, ...), custom_call_target="tpu_custom_call" | custom-call | tf_op jit(solution)/shard_map/pallas_call | solution.py:228
  88.9 3.1 %collective-permute-start.20 = (bf16[4,288,256]{2,1,0:T(8,128)(2,1)}, bf16[4,288,256]{2,1,0:T(8,128)(2,1)S(1)}, u32[]{:S(2)}, u32[]{:S(2)}) collective-permute-start(bf16[4,288,256]{2,1,0:T(8,128)(2,1)} %get-tuple-element.64), channel_id=1, source_target_pairs={{4,0},{8,4},{12,8},{16,12},{20,16},{24,20},{28,24},{5,1},{9,5},{13... | collective-permute-start | bytes 1769480 | tf_op jit(solution)/shard_map/ppermute | solution.py:179
  92.8 5.7 %shard_map.86 = (bf16[4,192,256]{2,1,0:T(8,128)(2,1)}, bf16[4,192,256]{2,1,0:T(8,128)(2,1)}, f32[4,192,256]{2,1,0:T(8,128)}) custom-call(bf16[208,512]{1,0:T(8,128)(2,1)} %get-tuple-element.36.refs_0_, bf16[208,512]{1,0:T(8,128)(2,1)} %copy-done.13, bf16[208,512]{1,0:T(8,128)(2,1)} %copy-done.14, bf16[208,512]{1,0:T(8,128)(2,1)} %copy-done.15, ...), custom_call_target="tpu_custom_call" | custom-call | tf_op jit(solution)/shard_map/pallas_call | solution.py:228
  98.5 2.1 %collective-permute-start.4 = (bf16[4,192,256]{2,1,0:T(8,128)(2,1)}, bf16[4,192,256]{2,1,0:T(8,128)(2,1)S(1)}, u32[]{:S(2)}, u32[]{:S(2)}) collective-permute-start(bf16[4,192,256]{2,1,0:T(8,128)(2,1)} %get-tuple-element.42), channel_id=1, source_target_pairs={{4,0},{8,4},{12,8},{16,12},{20,16},{24,20},{28,24},{5,1},{9,5},{13... | collective-permute-start | bytes 1179656 | tf_op jit(solution)/shard_map/ppermute | solution.py:179
  101.4 2.7 %shard_map.90 = (bf16[288,512]{1,0:T(8,128)(2,1)}, bf16[288,512]{1,0:T(8,128)(2,1)}, bf16[288,512]{1,0:T(8,128)(2,1)}, bf16[288,512]{1,0:T(8,128)(2,1)}) custom-call(bf16[4,288,256]{2,1,0:T(8,128)(2,1)} %get-tuple-element.51.near_ref, f32[4,288,256]{2,1,0:T(8,128)} %get-tuple-element.52.own_ref, bf16[4,288,256]{2,1,0:T(8,128)(2,1)} %copy-done.10), custom_call_target="tpu_custom_call" | custom-call | tf_op jit(solution)/shard_map/pallas_call | solution.py:30
  106.1 2.7 %shard_map.93 = (bf16[288,512]{1,0:T(8,128)(2,1)}, bf16[288,512]{1,0:T(8,128)(2,1)}, bf16[288,512]{1,0:T(8,128)(2,1)}, bf16[288,512]{1,0:T(8,128)(2,1)}) custom-call(bf16[4,288,256]{2,1,0:T(8,128)(2,1)} %get-tuple-element.62.near_ref, f32[4,288,256]{2,1,0:T(8,128)} %get-tuple-element.63.own_ref, bf16[4,288,256]{2,1,0:T(8,128)(2,1)} %copy-done.11), custom_call_target="tpu_custom_call" | custom-call | tf_op jit(solution)/shard_map/pallas_call | solution.py:30
  115.5 2.3 %shard_map.87 = (bf16[192,512]{1,0:T(8,128)(2,1)}, bf16[192,512]{1,0:T(8,128)(2,1)}, bf16[192,512]{1,0:T(8,128)(2,1)}, bf16[192,512]{1,0:T(8,128)(2,1)}) custom-call(bf16[4,192,256]{2,1,0:T(8,128)(2,1)} %get-tuple-element.40.near_ref, f32[4,192,256]{2,1,0:T(8,128)} %get-tuple-element.41.own_ref, bf16[4,192,256]{2,1,0:T(8,128)(2,1)} %copy-done.17), custom_call_target="tpu_custom_call" | custom-call | tf_op jit(solution)/shard_map/pallas_call | solution.py:30
  117.8 2.7 %collective-permute-done.21.refs_2_ = bf16[288,512]{1,0:T(8,128)(2,1)S(1)} collective-permute-done((bf16[288,512]{1,0:T(8,128)(2,1)}, bf16[288,512]{1,0:T(8,128)(2,1)S(1)}, u32[]{:S(2)}, u32[]{:S(2)}) %collective-permute-start.21) | collective-permute-done | bytes 294944 | tf_op jit(solution)/shard_map/ppermute | solution.py:185
  122.4 4.9 %collective-permute-done.23.refs_4_ = bf16[288,512]{1,0:T(8,128)(2,1)S(1)} collective-permute-done((bf16[288,512]{1,0:T(8,128)(2,1)}, bf16[288,512]{1,0:T(8,128)(2,1)S(1)}, u32[]{:S(2)}, u32[]{:S(2)}) %collective-permute-start.23) | collective-permute-done | bytes 294944 | tf_op jit(solution)/shard_map/ppermute | solution.py:185
  130.2 4.9 %shard_map.94.refs_5_ = bf16[1536,512]{1,0:T(8,128)(2,1)} custom-call(s32[1536,128]{1,0:T(8,128)} %broadcast_in_dim.5.refs_0_, bf16[288,512]{1,0:T(8,128)(2,1)} %get-tuple-element.65.refs_1_, bf16[288,512]{1,0:T(8,128)(2,1)} %copy-done.19, bf16[288,512]{1,0:T(8,128)(2,1)} %copy-done.21, bf16[288,512]{1,0:T(8,128)(2,1)} %copy-done.22), custom_call_target="tpu_custom_call" | custom-call | tf_op jit(solution)/shard_map/pallas_call | solution.py:30
  135.1 7.8 %collective-permute-done.14.refs_3_ = bf16[288,512]{1,0:T(8,128)(2,1)S(1)} collective-permute-done((bf16[288,512]{1,0:T(8,128)(2,1)S(1)}, bf16[288,512]{1,0:T(8,128)(2,1)S(1)}, u32[]{:S(2)}, u32[]{:S(2)}) %collective-permute-start.14) | collective-permute-done | bytes 294944 | tf_op jit(solution)/shard_map/ppermute | solution.py:185
  143.7 5.4 %shard_map.95.refs_5_ = bf16[1536,512]{1,0:T(8,128)(2,1)} custom-call(s32[1536,128]{1,0:T(8,128)} %broadcast_in_dim.5.refs_0_, bf16[288,512]{1,0:T(8,128)(2,1)} %get-tuple-element.54.refs_1_, bf16[288,512]{1,0:T(8,128)(2,1)} %copy-done.18, bf16[288,512]{1,0:T(8,128)(2,1)} %copy-done.20, bf16[288,512]{1,0:T(8,128)(2,1)} %copy-done.23, ...), custom_call_target="tpu_custom_call", output_to_operand_aliasing={{}: (5, {})} | custom-call | tf_op jit(solution)/shard_map/pallas_call | solution.py:30
  149.9 4.6 %shard_map.96 = bf16[1536,512]{1,0:T(8,128)(2,1)} custom-call(s32[1536,128]{1,0:T(8,128)} %broadcast_in_dim.5.refs_0_, bf16[192,512]{1,0:T(8,128)(2,1)} %get-tuple-element.43.refs_1_, bf16[192,512]{1,0:T(8,128)(2,1)} %copy-done.24, bf16[192,512]{1,0:T(8,128)(2,1)} %copy-done.25, bf16[192,512]{1,0:T(8,128)(2,1)} %copy-done.26, ...), custom_call_target="tpu_custom_call", output_to_operand_aliasing={{}: (5, {})} | custom-call | tf_op jit(solution)/shard_map/pallas_call | solution.py:30
  156.6 2.4 %slice_bitcast_fusion = bf16[192,8,384]{2,1,0:T(8,128)(2,1)} fusion(bf16[1536,512]{1,0:T(8,128)(2,1)} %shard_map.96), kind=kLoop, calls=%fused_computation | loop fusion | bytes 2359296 | tf_op jit(solution)/shard_map/reshape | solution.py:260
  (132 shorter events, 46.8 us)
Async XLA Ops:
  10.9 51.1 %collective-permute-start = (bf16[208,512]{1,0:T(8,128)(2,1)}, bf16[208,512]{1,0:T(8,128)(2,1)S(1)}, u32[]{:S(2)}, u32[]{:S(2)}) collective-permute-start(bf16[208,512]{1,0:T(8,128)(2,1)} %get-tuple-element.37), channel_id=1, source_target_pairs={{0,1},{1,0},{2,3},{3,2},{4,5},{5,4},{6,7},{7,6},{8,9},{9,8},{10,11... | collective-permute-start | bytes 638984 | tf_op jit(solution)/shard_map/ppermute | solution.py:185
  12.4 49.6 %collective-permute-start.1 = (bf16[208,512]{1,0:T(8,128)(2,1)}, bf16[208,512]{1,0:T(8,128)(2,1)S(1)}, u32[]{:S(2)}, u32[]{:S(2)}) collective-permute-start(bf16[208,512]{1,0:T(8,128)(2,1)} %get-tuple-element.38), channel_id=1, source_target_pairs={{0,2},{1,3},{2,0},{3,1},{4,6},{5,7},{6,4},{7,5},{8,10},{9,11},{10,... | collective-permute-start | bytes 638984 | tf_op jit(solution)/shard_map/ppermute | solution.py:185
  13.9 48.0 %collective-permute-start.2 = (bf16[208,512]{1,0:T(8,128)(2,1)}, bf16[208,512]{1,0:T(8,128)(2,1)S(1)}, u32[]{:S(2)}, u32[]{:S(2)}) collective-permute-start(bf16[208,512]{1,0:T(8,128)(2,1)} %get-tuple-element.39), channel_id=1, source_target_pairs={{0,3},{1,2},{2,1},{3,0},{4,7},{5,6},{6,5},{7,4},{8,11},{9,10},{10,... | collective-permute-start | bytes 638984 | tf_op jit(solution)/shard_map/ppermute | solution.py:185
  19.5 17.8 %collective-permute-start.9 = (bf16[304,512]{1,0:T(8,128)(2,1)}, bf16[304,512]{1,0:T(8,128)(2,1)S(1)}, u32[]{:S(2)}, u32[]{:S(2)}) collective-permute-start(bf16[304,512]{1,0:T(8,128)(2,1)} %get-tuple-element.49), channel_id=1, source_target_pairs={{0,2},{1,3},{2,0},{3,1},{4,6},{5,7},{6,4},{7,5},{8,10},{9,11},{10,... | collective-permute-start | bytes 933896 | tf_op jit(solution)/shard_map/ppermute | solution.py:185
  21.0 9.4 %collective-permute-start.10 = (bf16[304,512]{1,0:T(8,128)(2,1)}, bf16[304,512]{1,0:T(8,128)(2,1)S(1)}, u32[]{:S(2)}, u32[]{:S(2)}) collective-permute-start(bf16[304,512]{1,0:T(8,128)(2,1)} %get-tuple-element.50), channel_id=1, source_target_pairs={{0,3},{1,2},{2,1},{3,0},{4,7},{5,6},{6,5},{7,4},{8,11},{9,10},{10,... | collective-permute-start | bytes 933896 | tf_op jit(solution)/shard_map/ppermute | solution.py:185
  30.4 8.3 %collective-permute-start.8 = (bf16[304,512]{1,0:T(8,128)(2,1)S(1)}, bf16[304,512]{1,0:T(8,128)(2,1)S(1)}, u32[]{:S(2)}, u32[]{:S(2)}) collective-permute-start(bf16[304,512]{1,0:T(8,128)(2,1)S(1)} %copy-done.28), channel_id=1, source_target_pairs={{0,1},{1,0},{2,3},{3,2},{4,5},{5,4},{6,7},{7,6},{8,9},{9,8},{10,11... | collective-permute-start | bytes 933896 | tf_op jit(solution)/shard_map/ppermute | solution.py:185
  37.2 11.3 %collective-permute-start.18 = (bf16[304,512]{1,0:T(8,128)(2,1)}, bf16[304,512]{1,0:T(8,128)(2,1)S(1)}, u32[]{:S(2)}, u32[]{:S(2)}) collective-permute-start(bf16[304,512]{1,0:T(8,128)(2,1)} %get-tuple-element.61), channel_id=1, source_target_pairs={{0,3},{1,2},{2,1},{3,0},{4,7},{5,6},{6,5},{7,4},{8,11},{9,10},{10,... | collective-permute-start | bytes 933896 | tf_op jit(solution)/shard_map/ppermute | solution.py:185
  38.8 19.3 %collective-permute-start.16 = (bf16[304,512]{1,0:T(8,128)(2,1)}, bf16[304,512]{1,0:T(8,128)(2,1)S(1)}, u32[]{:S(2)}, u32[]{:S(2)}) collective-permute-start(bf16[304,512]{1,0:T(8,128)(2,1)} %get-tuple-element.59), channel_id=1, source_target_pairs={{0,1},{1,0},{2,3},{3,2},{4,5},{5,4},{6,7},{7,6},{8,9},{9,8},{10,11... | collective-permute-start | bytes 933896 | tf_op jit(solution)/shard_map/ppermute | solution.py:185
  48.6 7.5 %collective-permute-start.17 = (bf16[304,512]{1,0:T(8,128)(2,1)S(1)}, bf16[304,512]{1,0:T(8,128)(2,1)S(1)}, u32[]{:S(2)}, u32[]{:S(2)}) collective-permute-start(bf16[304,512]{1,0:T(8,128)(2,1)S(1)} %copy-done.27), channel_id=1, source_target_pairs={{0,2},{1,3},{2,0},{3,1},{4,6},{5,7},{6,4},{7,5},{8,10},{9,11},{10,... | collective-permute-start | bytes 933896 | tf_op jit(solution)/shard_map/ppermute | solution.py:185
  56.1 11.5 %collective-permute-start.11 = (bf16[4,304,256]{2,1,0:T(8,128)(2,1)S(1)}, bf16[4,304,256]{2,1,0:T(8,128)(2,1)S(1)}, u32[]{:S(2)}, u32[]{:S(2)}) collective-permute-start(bf16[4,304,256]{2,1,0:T(8,128)(2,1)S(1)} %pad_maximum_fusion), channel_id=1, source_target_pairs={{0,4},{4,8},{8,12},{12,16},{16,20},{20,24},{24,28},{1,5},{5,9},{9,... | collective-permute-start | bytes 1867784 | tf_op jit(solution)/shard_map/ppermute | solution.py:179
  58.2 22.2 %collective-permute-start.19 = (bf16[4,304,256]{2,1,0:T(8,128)(2,1)S(1)}, bf16[4,304,256]{2,1,0:T(8,128)(2,1)S(1)}, u32[]{:S(2)}, u32[]{:S(2)}) collective-permute-start(bf16[4,304,256]{2,1,0:T(8,128)(2,1)S(1)} %pad_maximum_fusion.1), channel_id=1, source_target_pairs={{0,4},{4,8},{8,12},{12,16},{16,20},{20,24},{24,28},{1,5},{5,9},{9,... | collective-permute-start | bytes 1867784 | tf_op jit(solution)/shard_map/ppermute | solution.py:179
  76.0 24.6 %collective-permute-start.12 = (bf16[4,288,256]{2,1,0:T(8,128)(2,1)}, bf16[4,288,256]{2,1,0:T(8,128)(2,1)S(1)}, u32[]{:S(2)}, u32[]{:S(2)}) collective-permute-start(bf16[4,288,256]{2,1,0:T(8,128)(2,1)} %get-tuple-element.53), channel_id=1, source_target_pairs={{4,0},{8,4},{12,8},{16,12},{20,16},{24,20},{28,24},{5,1},{9,5},{13... | collective-permute-start | bytes 1769480 | tf_op jit(solution)/shard_map/ppermute | solution.py:179
  78.0 14.0 %collective-permute-start.3 = (bf16[4,208,256]{2,1,0:T(8,128)(2,1)S(1)}, bf16[4,208,256]{2,1,0:T(8,128)(2,1)S(1)}, u32[]{:S(2)}, u32[]{:S(2)}) collective-permute-start(bf16[4,208,256]{2,1,0:T(8,128)(2,1)S(1)} %pad_maximum_fusion.2), channel_id=1, source_target_pairs={{0,4},{4,8},{8,12},{12,16},{16,20},{20,24},{24,28},{1,5},{5,9},{9,... | collective-permute-start | bytes 1277960 | tf_op jit(solution)/shard_map/ppermute | solution.py:179
  88.9 16.5 %collective-permute-start.20 = (bf16[4,288,256]{2,1,0:T(8,128)(2,1)}, bf16[4,288,256]{2,1,0:T(8,128)(2,1)S(1)}, u32[]{:S(2)}, u32[]{:S(2)}) collective-permute-start(bf16[4,288,256]{2,1,0:T(8,128)(2,1)} %get-tuple-element.64), channel_id=1, source_target_pairs={{4,0},{8,4},{12,8},{16,12},{20,16},{24,20},{28,24},{5,1},{9,5},{13... | collective-permute-start | bytes 1769480 | tf_op jit(solution)/shard_map/ppermute | solution.py:179
  98.5 13.9 %collective-permute-start.4 = (bf16[4,192,256]{2,1,0:T(8,128)(2,1)}, bf16[4,192,256]{2,1,0:T(8,128)(2,1)S(1)}, u32[]{:S(2)}, u32[]{:S(2)}) collective-permute-start(bf16[4,192,256]{2,1,0:T(8,128)(2,1)} %get-tuple-element.42), channel_id=1, source_target_pairs={{4,0},{8,4},{12,8},{16,12},{20,16},{24,20},{28,24},{5,1},{9,5},{13... | collective-permute-start | bytes 1179656 | tf_op jit(solution)/shard_map/ppermute | solution.py:179
  104.1 10.0 %collective-permute-start.13 = (bf16[288,512]{1,0:T(8,128)(2,1)}, bf16[288,512]{1,0:T(8,128)(2,1)S(1)}, u32[]{:S(2)}, u32[]{:S(2)}) collective-permute-start(bf16[288,512]{1,0:T(8,128)(2,1)} %get-tuple-element.55), channel_id=1, source_target_pairs={{0,1},{1,0},{2,3},{3,2},{4,5},{5,4},{6,7},{7,6},{8,9},{9,8},{10,11... | collective-permute-start | bytes 884744 | tf_op jit(solution)/shard_map/ppermute | solution.py:185
  108.8 11.6 %collective-permute-start.21 = (bf16[288,512]{1,0:T(8,128)(2,1)}, bf16[288,512]{1,0:T(8,128)(2,1)S(1)}, u32[]{:S(2)}, u32[]{:S(2)}) collective-permute-start(bf16[288,512]{1,0:T(8,128)(2,1)} %get-tuple-element.66), channel_id=1, source_target_pairs={{0,1},{1,0},{2,3},{3,2},{4,5},{5,4},{6,7},{7,6},{8,9},{9,8},{10,11... | collective-permute-start | bytes 884744 | tf_op jit(solution)/shard_map/ppermute | solution.py:185
  109.6 12.0 %collective-permute-start.22 = (bf16[288,512]{1,0:T(8,128)(2,1)}, bf16[288,512]{1,0:T(8,128)(2,1)S(1)}, u32[]{:S(2)}, u32[]{:S(2)}) collective-permute-start(bf16[288,512]{1,0:T(8,128)(2,1)} %get-tuple-element.67), channel_id=1, source_target_pairs={{0,2},{1,3},{2,0},{3,1},{4,6},{5,7},{6,4},{7,5},{8,10},{9,11},{10,... | collective-permute-start | bytes 884744 | tf_op jit(solution)/shard_map/ppermute | solution.py:185
  110.6 16.7 %collective-permute-start.23 = (bf16[288,512]{1,0:T(8,128)(2,1)}, bf16[288,512]{1,0:T(8,128)(2,1)S(1)}, u32[]{:S(2)}, u32[]{:S(2)}) collective-permute-start(bf16[288,512]{1,0:T(8,128)(2,1)} %get-tuple-element.68), channel_id=1, source_target_pairs={{0,3},{1,2},{2,1},{3,0},{4,7},{5,6},{6,5},{7,4},{8,11},{9,10},{10,... | collective-permute-start | bytes 884744 | tf_op jit(solution)/shard_map/ppermute | solution.py:185
  112.3 30.6 %collective-permute-start.14 = (bf16[288,512]{1,0:T(8,128)(2,1)S(1)}, bf16[288,512]{1,0:T(8,128)(2,1)S(1)}, u32[]{:S(2)}, u32[]{:S(2)}) collective-permute-start(bf16[288,512]{1,0:T(8,128)(2,1)S(1)} %copy-done.30), channel_id=1, source_target_pairs={{0,2},{1,3},{2,0},{3,1},{4,6},{5,7},{6,4},{7,5},{8,10},{9,11},{10,... | collective-permute-start | bytes 884744 | tf_op jit(solution)/shard_map/ppermute | solution.py:185
  114.1 28.8 %collective-permute-start.15 = (bf16[288,512]{1,0:T(8,128)(2,1)S(1)}, bf16[288,512]{1,0:T(8,128)(2,1)S(1)}, u32[]{:S(2)}, u32[]{:S(2)}) collective-permute-start(bf16[288,512]{1,0:T(8,128)(2,1)S(1)} %copy-done.29), channel_id=1, source_target_pairs={{0,3},{1,2},{2,1},{3,0},{4,7},{5,6},{6,5},{7,4},{8,11},{9,10},{10,... | collective-permute-start | bytes 884744 | tf_op jit(solution)/shard_map/ppermute | solution.py:185
  120.4 28.7 %collective-permute-start.5 = (bf16[192,512]{1,0:T(8,128)(2,1)}, bf16[192,512]{1,0:T(8,128)(2,1)S(1)}, u32[]{:S(2)}, u32[]{:S(2)}) collective-permute-start(bf16[192,512]{1,0:T(8,128)(2,1)} %get-tuple-element.44), channel_id=1, source_target_pairs={{0,1},{1,0},{2,3},{3,2},{4,5},{5,4},{6,7},{7,6},{8,9},{9,8},{10,11... | collective-permute-start | bytes 589832 | tf_op jit(solution)/shard_map/ppermute | solution.py:185
  121.7 27.5 %collective-permute-start.6 = (bf16[192,512]{1,0:T(8,128)(2,1)}, bf16[192,512]{1,0:T(8,128)(2,1)S(1)}, u32[]{:S(2)}, u32[]{:S(2)}) collective-permute-start(bf16[192,512]{1,0:T(8,128)(2,1)} %get-tuple-element.45), channel_id=1, source_target_pairs={{0,2},{1,3},{2,0},{3,1},{4,6},{5,7},{6,4},{7,5},{8,10},{9,11},{10,... | collective-permute-start | bytes 589832 | tf_op jit(solution)/shard_map/ppermute | solution.py:185
  127.3 21.9 %collective-permute-start.7 = (bf16[192,512]{1,0:T(8,128)(2,1)}, bf16[192,512]{1,0:T(8,128)(2,1)S(1)}, u32[]{:S(2)}, u32[]{:S(2)}) collective-permute-start(bf16[192,512]{1,0:T(8,128)(2,1)} %get-tuple-element.46), channel_id=1, source_target_pairs={{0,3},{1,2},{2,1},{3,0},{4,7},{5,6},{6,5},{7,4},{8,11},{9,10},{10,... | collective-permute-start | bytes 589832 | tf_op jit(solution)/shard_map/ppermute | solution.py:185
  (31 other events, 305.3 us)

commit v2 on v1

v2 whole, which is shorter than its diff:
```python
from functools import partial

import jax
import jax.numpy as jnp
from jax import lax
from jax.experimental import pallas as pl
from jax.experimental.pallas import tpu as pltpu
from jax.sharding import PartitionSpec as P

H = 64
CAP = 48
MASKED = -1e30
DOC_ROWS = 16
DOC_LANES = 64
PARTS = (6, 6, 4)
KERNEL_BYTES = 20 * 1024 * 1024
TOGETHER = 2

VMEM = pl.BlockSpec(memory_space=pltpu.VMEM)


def head_chunks(heads):
    total = sum(PARTS)
    edges = [0]
    for i in range(len(PARTS)):
        edges.append(round(heads * sum(PARTS[: i + 1]) / total))
    return [(a, b - a) for a, b in zip(edges[:-1], edges[1:]) if b > a]


def call(kernel, out_shape, *operands, after=(), scratch=(), in_specs=None, pairs=0):
    waits = len(after)
    specs = in_specs or [VMEM] * len(operands)

    def body(*refs):
        kernel(*refs[waits:])

    return pl.pallas_call(
        body,
        out_shape=out_shape,
        in_specs=[pl.BlockSpec(memory_space=pl.ANY)] * waits + specs,
        out_specs=jax.tree.map(lambda _: VMEM, out_shape),
        scratch_shapes=list(scratch),
        cost_estimate=pl.CostEstimate(flops=6 * 10**9, bytes_accessed=20 * 10**6, transcendentals=0),
        compiler_params=pltpu.CompilerParams(vmem_limit_bytes=KERNEL_BYTES + 40 * pairs),
    )(*after, *operands)


def dot(a, b, dims):
    return lax.dot_general(a, b, (dims, ((), ())), preferred_element_type=jnp.float32)


NN = ((1,), (0,))
NT = ((1,), (1,))
TN = ((0,), (0,))


def one_hot(index, base, size, shape, dim):
    middle = size // 2
    near = jnp.clip(index - base, -1, size) - middle
    near = near.astype(jnp.float32).astype(jnp.bfloat16)
    spot = lax.broadcasted_iota(jnp.int32, tuple(n if i == dim else 1 for i, n in enumerate(shape)), dim)
    spot = (spot - middle).astype(jnp.float32).astype(jnp.bfloat16)
    one, zero = jnp.ones((), jnp.bfloat16), jnp.zeros((), jnp.bfloat16)
    return jnp.where(jnp.broadcast_to(near, shape) == jnp.broadcast_to(spot, shape), one, zero)


def spread(values):
    top, tokens = values.shape
    wide = jnp.broadcast_to(values.T[:, None, :], (tokens, top, top))
    return wide.reshape(tokens * top, top)


def own_route(routes, top):
    return lax.broadcasted_iota(jnp.int32, (routes, top), 1) == (
        lax.broadcasted_iota(jnp.int32, (routes, top), 0) % top
    )


def route_column(values):
    top, tokens = values.shape
    own = own_route(tokens * top, top)
    return jnp.sum(jnp.where(own, spread(values), 0.0), axis=1, keepdims=True)


def sigmoid(x):
    return 1.0 / (1.0 + jnp.exp(-x))


def prepare_kernel(heads_ref, slots_ref, logits_ref, doc_lengths_ref, proj_ref, cot_ref,
                   flat_ref, column_ref, docs_ref, rows_ref):
    top, tokens = heads_ref.shape
    routes = tokens * top
    width = proj_ref.shape[1]
    gate = route_column(sigmoid(logits_ref[...]))
    rows_ref[:, :width] = proj_ref[...]
    rows_ref[:, width:] = (cot_ref[...].astype(jnp.float32) * gate).astype(jnp.bfloat16)
    slots = route_column((heads_ref[...] * CAP + slots_ref[...]).astype(jnp.float32))
    slots = jnp.broadcast_to(slots, (routes, 128))
    column_ref[...] = slots.astype(jnp.int32)
    flat_ref[...] = slots.T[:8].astype(jnp.int32)
    place = lax.axis_index("seq") * lax.axis_size("head") + lax.axis_index("head")
    position = place * tokens + lax.broadcasted_iota(jnp.int32, docs_ref.shape, 1) // top
    docs = jnp.ones(docs_ref.shape, jnp.float32)
    end = 0
    for i in range(doc_lengths_ref.shape[0]):
        end = end + doc_lengths_ref[i]
        docs = docs + jnp.where(position >= end, 1.0, 0.0)
    docs_ref[...] = docs


def dispatch_kernel(first, count, owned, groups, flat_ref, docs_ref, rows_ref, *refs):
    out_refs = refs[:groups]
    hot_ref = refs[groups]
    me = lax.axis_index("head")
    rows = count * CAP
    routes, width = rows_ref.shape
    head_size = width // 4
    flat = flat_ref[0:1, :]
    docs = docs_ref[0:1, :].astype(jnp.bfloat16)
    lane = lax.broadcasted_iota(jnp.int32, (CAP, DOC_LANES), 1)
    for d, out_ref in enumerate(out_refs):
        base = ((me ^ d) * owned + first) * CAP
        hot = one_hot(flat, base, rows, (rows, routes), 0)
        hot_ref[d * rows : (d + 1) * rows, :] = hot
        marked = hot * docs
        slot_docs = marked[:, :128]
        for i in range(128, routes, 128):
            slot_docs = slot_docs + marked[:, i : i + 128]
        slot_docs = jnp.sum(slot_docs.astype(jnp.float32), axis=1, keepdims=True)
        table = jnp.zeros((CAP, DOC_LANES), jnp.float32)
        for h in range(count):
            table = jnp.where(lane == h, slot_docs[h * CAP : (h + 1) * CAP], table)
        thirds = [table[i * DOC_ROWS : (i + 1) * DOC_ROWS] for i in range(CAP // DOC_ROWS)]
        packed = jnp.concatenate(thirds + [jnp.zeros_like(thirds[0])], 1)
        blank = jnp.zeros((DOC_ROWS, head_size), jnp.float32)
        out_ref[rows:, :] = jnp.concatenate([blank, packed, blank], 1).astype(jnp.bfloat16)
    taken = dot(hot_ref[...], rows_ref[...], NN).astype(jnp.bfloat16)
    for d, out_ref in enumerate(out_refs):
        out_ref[:rows, :] = taken[d * rows : (d + 1) * rows]


def doc_table(packed):
    packed = packed.astype(jnp.float32)
    thirds = [packed[:, i * DOC_LANES : (i + 1) * DOC_LANES] for i in range(CAP // DOC_ROWS)]
    return jnp.concatenate(thirds, 0)


def attention_kernel(count, groups, *refs):
    blocks = refs[:groups]
    before_ref = refs[groups]
    near_ref, far_ref, own_ref, mask_ref = refs[groups + 1 :]
    me = lax.axis_index("head")
    rows = count * CAP
    head_size = blocks[0].shape[1] // 4
    scaling = head_size ** (-0.5)
    span = groups * CAP
    query_docs = jnp.concatenate(
        [doc_table(b[rows:, head_size : 3 * head_size]) for b in blocks], 0
    )
    before_docs = jnp.concatenate([doc_table(before_ref[d, rows:, :]) for d in range(groups)], 0)
    key_docs = jnp.concatenate([before_docs, query_docs], 0)
    key_docs = jnp.concatenate([key_docs, jnp.zeros_like(key_docs)], 1).T

    def order(index):
        return (me ^ (index // CAP)) * CAP + index % CAP

    row_order = order(lax.broadcasted_iota(jnp.int32, (span, 1), 0))
    column = lax.broadcasted_iota(jnp.int32, (1, 2 * span), 1)
    column_order = jnp.where(column < span, -1, order(jnp.maximum(column - span, 0)))
    mask_ref[...] = jnp.where(column_order <= row_order, 0.0, MASKED)

    def piece(h, i):
        here, part = slice(h * CAP, (h + 1) * CAP), slice(i * head_size, (i + 1) * head_size)
        return jnp.concatenate([b[here, part] for b in blocks], 0)

    def both(h, i):
        here, part = slice(h * CAP, (h + 1) * CAP), slice(i * head_size, (i + 1) * head_size)
        earlier = [before_ref[d, here, part] for d in range(groups)]
        return jnp.concatenate(earlier + [piece(h, i + 1)], 0)

    for start in range(0, count, TOGETHER):
        heads = range(start, min(start + TOGETHER, count))
        queries = [piece(h, 0) for h in heads]
        grads_out = [piece(h, 3) for h in heads]
        key_rows = [both(h, 0) for h in heads]
        value_rows = [both(h, 1) for h in heads]
        scores = [dot(q, k, NT) for q, k in zip(queries, key_rows)]
        weight_grads = [dot(g, v, NT) for g, v in zip(grads_out, value_rows)]
        weights = []
        for h, s in zip(heads, scores):
            s = s * scaling + mask_ref[...]
            s = jnp.where(key_docs[h : h + 1, :] == query_docs[:, h : h + 1], s, MASKED)
            powers = jnp.exp(s - jnp.max(s, axis=1, keepdims=True))
            weights.append(powers * (1.0 / jnp.sum(powers, axis=1, keepdims=True)))
        weights_low = [w.astype(jnp.bfloat16) for w in weights]
        attended = [dot(w, v, NN).astype(jnp.bfloat16) for w, v in zip(weights_low, value_rows)]
        value_grads = [dot(w, g, TN) for w, g in zip(weights_low, grads_out)]
        deltas = [
            jnp.sum(g.astype(jnp.float32) * a.astype(jnp.float32), axis=1, keepdims=True)
            for g, a in zip(grads_out, attended)
        ]
        score_grads = [
            (w * (wg - d)).astype(jnp.bfloat16) for w, wg, d in zip(weights, weight_grads, deltas)
        ]
        query_grads = [
            (dot(s, k, NN) * scaling).astype(jnp.bfloat16) for s, k in zip(score_grads, key_rows)
        ]
        key_grads = [dot(s, q, TN) * scaling for s, q in zip(score_grads, queries)]
        for i, h in enumerate(heads):
            here = slice(h * CAP, (h + 1) * CAP)
            for d in range(groups):
                part = slice(d * CAP, (d + 1) * CAP)
                own = slice(span + d * CAP, span + (d + 1) * CAP)
                near_ref[d, here, :head_size] = attended[i][part]
                near_ref[d, here, head_size:] = query_grads[i][part]
                far_ref[d, here, :head_size] = key_grads[i][part].astype(jnp.bfloat16)
                far_ref[d, here, head_size:] = value_grads[i][part].astype(jnp.bfloat16)
                own_ref[d, here, :head_size] = key_grads[i][own]
                own_ref[d, here, head_size:] = value_grads[i][own]


def combine_kernel(groups, near_ref, own_ref, incoming_ref, *out_refs):
    half = near_ref.shape[2]
    for d in range(groups):
        out_refs[d][:, :half] = near_ref[d]
        total = own_ref[d] + incoming_ref[d].astype(jnp.float32)
        out_refs[d][:, half:] = total.astype(jnp.bfloat16)


def routed(first, count, owned, groups, refs):
    column_ref = refs[0]
    blocks = refs[1 : groups + 1]
    hot_ref = refs[-1]
    me = lax.axis_index("head")
    rows = count * CAP
    routes = column_ref.shape[0]
    for d in range(groups):
        base = ((me ^ d) * owned + first) * CAP
        hot = one_hot(column_ref[:, 0:1], base, rows, (routes, rows), 1)
        hot_ref[:, d * rows : (d + 1) * rows] = hot
    return dot(hot_ref[...], jnp.concatenate([b[...] for b in blocks], 0), NN)


def return_kernel(first, count, owned, groups, initial, *refs):
    taken = routed(first, count, owned, groups, refs)
    if not initial:
        taken = taken + refs[groups + 1][...].astype(jnp.float32)
    refs[-2][...] = taken.astype(jnp.bfloat16)


def finish_kernel(first, count, owned, groups, initial, *refs):
    logits_ref, cot_ref, heads_out_ref, proj_grads_ref, gate_grads_ref = refs[-6:-1]
    taken = routed(first, count, owned, groups, refs)
    if not initial:
        taken = taken + refs[groups + 1][...].astype(jnp.float32)
    head_size = cot_ref.shape[1]
    top, tokens = logits_ref.shape
    routes = tokens * top
    proj_grads_ref[...] = taken[:, head_size:].astype(jnp.bfloat16)
    attended = taken[:, :head_size]
    gate_table = sigmoid(logits_ref[...])
    heads_out_ref[...] = (attended * route_column(gate_table)).astype(jnp.bfloat16)
    sums = jnp.sum(cot_ref[...].astype(jnp.float32) * attended, axis=1, keepdims=True)
    sums = jnp.where(own_route(routes, top), sums, 0.0).reshape(tokens, top, top)
    gate_grads_ref[...] = jnp.sum(sums, axis=1).T * gate_table * (1.0 - gate_table)


def shifted(block, axis, distance):
    devices = range(lax.axis_size(axis))
    route = [(i, i + distance) for i in devices if i + distance in devices]
    return lax.ppermute(block, axis, route)


def exchanged(blocks):
    groups = len(blocks)
    return [blocks[0]] + [
        lax.ppermute(blocks[d], "head", [(i, i ^ d) for i in range(groups)])
        for d in range(1, groups)
    ]


def per_device(projections, routed_heads, slot_index, gate_logits, doc_lengths, cotangent):
    tokens, top, width = projections.shape
    head_size = width // 3
    routes = tokens * top
    groups = lax.axis_size("head")
    owned = H // groups
    bf16, f32 = jnp.bfloat16, jnp.float32

    shape = jax.ShapeDtypeStruct
    logits = gate_logits.T
    cot_rows = cotangent.reshape(routes, head_size)
    flat, columns, documents, rows_in = call(
        prepare_kernel,
        [
            shape((8, routes), jnp.int32),
            shape((routes, 128), jnp.int32),
            shape((8, routes), f32),
            shape((routes, width + head_size), bf16),
        ],
        routed_heads.T,
        slot_index.T,
        logits,
        doc_lengths,
        projections.reshape(routes, width),
        cot_rows,
        in_specs=[VMEM] * 3 + [pl.BlockSpec(memory_space=pltpu.SMEM)] + [VMEM] * 2,
    )

    chunks = head_chunks(owned)
    last = len(chunks) - 1
    blocks_out = []
    for first, count in chunks:
        rows = count * CAP
        sent = call(
            partial(dispatch_kernel, first, count, owned, groups),
            [shape((rows + DOC_ROWS, width + head_size), bf16)] * groups,
            flat,
            documents,
            rows_in,
            scratch=[pltpu.VMEM((groups * rows, routes), bf16)],
        )
        blocks_out.append(sent)
    received = [exchanged(sent) for sent in blocks_out]

    homes, fars = [], []
    for i, ((first, count), blocks) in enumerate(zip(chunks, received)):
        rows = count * CAP
        if i > 0:
            *blocks, fars[-1] = lax.optimization_barrier((*blocks, fars[-1]))
        else:
            waits = [sent[0] for sent in blocks_out[1:]]
            blocks = lax.optimization_barrier((*blocks, *waits))[: len(blocks)]
        before = shifted(jnp.stack([b[:, head_size : 3 * head_size] for b in blocks]), "seq", 1)
        if i > 0:
            homes.append(finish_chunk(fars[-1]))
        pair = (groups, rows, 2 * head_size)
        near, far, own = call(
            partial(attention_kernel, count, groups),
            [shape(pair, bf16), shape(pair, bf16), shape(pair, f32)],
            *blocks,
            before,
            after=homes[-1][:1] if homes else (),
            scratch=[pltpu.VMEM((groups * CAP, 2 * groups * CAP), f32)],
            pairs=2 * (groups * CAP) ** 2,
        )
        fars.append(far)

        def finish_chunk(far, near=near, own=own, rows=rows):
            return call(
                partial(combine_kernel, groups),
                [shape((rows, 4 * head_size), bf16)] * groups,
                near,
                own,
                shifted(far, "seq", -1),
            )

    homes.append(finish_chunk(fars[-1]))
    total = []
    for i, ((first, count), home) in enumerate(zip(chunks, homes)):
        rows = count * CAP
        operands = [columns, *exchanged(home), *total]
        scratch = [pltpu.VMEM((routes, groups * rows), bf16)]
        if i < last:
            total = [
                call(
                    partial(return_kernel, first, count, owned, groups, i == 0),
                    shape((routes, 4 * head_size), bf16),
                    *operands,
                    after=[homes[i + 1][0]],
                    scratch=scratch,
                )
            ]
    head_outputs, projection_grads, gate_grads = call(
        partial(finish_kernel, first, count, owned, groups, last == 0),
        [
            shape((routes, head_size), bf16),
            shape((routes, width), bf16),
            shape(logits.shape, f32),
        ],
        *operands,
        logits,
        cot_rows,
        scratch=scratch,
    )
    return (
        head_outputs.reshape(tokens, top, head_size),
        projection_grads.reshape(tokens, top, width),
        gate_grads.T,
    )


def solution(mesh):
    return jax.shard_map(
        per_device,
        mesh=mesh,
        in_specs=(
            P(("seq", "head"), None, None),
            P(("seq", "head"), None),
            P(("seq", "head"), None),
            P(("seq", "head"), None),
            P(),
            P(("seq", "head"), None, None),
        ),
        out_specs=(
            P(("seq", "head"), None, None),
            P(("seq", "head"), None, None),
            P(("seq", "head"), None),
        ),
        check_vma=False,
    )
```

time: 161 us -> 106 us (0.66)
  the two profiles are of different devices: /device:TPU:16 before, /device:TPU:9 now
where the time goes in v2:
time: 106 us; the launch traced here: 105 us
  waiting for transfers between devices  39.5 us (37%)
  starting transfers between devices  34.5 us (33%)
  Pallas kernels  24.4 us (23%)
  local copies, waits for them, and re-layouts  5.14 us (5%)
    pallas_call x13, Pallas kernels, call(): pl.pallas_call(body, out_shape=out_shape, in_specs=[pl.BlockSpec(memory_s...  24.4 us
    ppermute x18, waiting for transfers between devices, exchanged(): lax.ppermute(blocks[d], 'head', [(i, i ^ d) for i in range(groups)])  21.5 us
    ppermute x6, starting transfers between devices, shifted(): return lax.ppermute(block, axis, route)  18.6 us
    ppermute x6, waiting for transfers between devices, shifted(): return lax.ppermute(block, axis, route)  18 us
    ppermute x18, starting transfers between devices, exchanged(): lax.ppermute(blocks[d], 'head', [(i, i ^ d) for i in range(groups)])  16 us
    unnamed x16, local copies, waits for them, and re-layouts  5.01 us
  transfers between devices with their start and end apart: 24, of which 13 were waited for; matrix products, arithmetic and copies ran while one was open for 0% of the time, Pallas kernels for 17%

profile of v2, /device:TPU:9, one launch (start us, length us, event | category | flops | bytes accessed | tf_op | source)
XLA Modules:
  0.0 104.7 jit_solution(12499617690960005822)
XLA Ops:
  5.6 1.4 %shard_map.85 = (s32[8,1536]{1,0:T(8,128)S(1)}, s32[1536,128]{1,0:T(8,128)S(1)}, f32[8,1536]{1,0:T(8,128)S(1)}, bf16[1536,512]{1,0:T(8,128)(2,1)S(1)}) custom-call(s32[8,192]{1,0:T(8,128)S(1)} %bitcast.35, s32[8,192]{1,0:T(8,128)S(1)} %bitcast.36, f32[8,192]{1,0:T(8,128)S(1)} %bitcast.37, s32[16]{0:T(128)S(1)} %copy-done.7, bf16[1536,384]{1,0:T(8,128)(2,1)S(1)} %bitcast.32, ...), custom_call_target="tpu_custom_call" | custom-call | flops 6000000000 | bytes 20000000 | tf_op jit(solution)/shard_map/pallas_call | solution.py:37
  7.1 2.0 %shard_map.86 = (bf16[304,512]{1,0:T(8,128)(2,1)S(1)}, bf16[304,512]{1,0:T(8,128)(2,1)S(1)}, bf16[304,512]{1,0:T(8,128)(2,1)S(1)}, bf16[304,512]{1,0:T(8,128)(2,1)S(1)}) custom-call(s32[8,1536]{1,0:T(8,128)S(1)} %get-tuple-element.58.refs_0_, f32[8,1536]{1,0:T(8,128)S(1)} %get-tuple-element.59.refs_1_, bf16[1536,512]{1,0:T(8,128)(2,1)S(1)} %get-tuple-element.60.refs_2_), custom_call_target="tpu_custom_call" | custom-call | flops 6000000000 | bytes 20000000 | tf_op jit(solution)/shard_map/pallas_call | solution.py:37
  11.8 1.4 %shard_map.88 = (bf16[208,512]{1,0:T(8,128)(2,1)S(1)}, bf16[208,512]{1,0:T(8,128)(2,1)S(1)}, bf16[208,512]{1,0:T(8,128)(2,1)S(1)}, bf16[208,512]{1,0:T(8,128)(2,1)S(1)}) custom-call(s32[8,1536]{1,0:T(8,128)S(1)} %get-tuple-element.58.refs_0_, f32[8,1536]{1,0:T(8,128)S(1)} %get-tuple-element.59.refs_1_, bf16[1536,512]{1,0:T(8,128)(2,1)S(1)} %get-tuple-element.60.refs_2_), custom_call_target="tpu_custom_call" | custom-call | flops 6000000000 | bytes 20000000 | tf_op jit(solution)/shard_map/pallas_call | solution.py:37
  13.2 2.0 %shard_map.87 = (bf16[304,512]{1,0:T(8,128)(2,1)S(1)}, bf16[304,512]{1,0:T(8,128)(2,1)S(1)}, bf16[304,512]{1,0:T(8,128)(2,1)S(1)}, bf16[304,512]{1,0:T(8,128)(2,1)S(1)}) custom-call(s32[8,1536]{1,0:T(8,128)S(1)} %get-tuple-element.58.refs_0_, f32[8,1536]{1,0:T(8,128)S(1)} %get-tuple-element.59.refs_1_, bf16[1536,512]{1,0:T(8,128)(2,1)S(1)} %get-tuple-element.60.refs_2_), custom_call_target="tpu_custom_call" | custom-call | flops 6000000000 | bytes 20000000 | tf_op jit(solution)/shard_map/pallas_call | solution.py:37
  15.2 2.2 %collective-permute-done.refs_1_ = bf16[304,512]{1,0:T(8,128)(2,1)S(1)} collective-permute-done((bf16[304,512]{1,0:T(8,128)(2,1)S(1)}, bf16[304,512]{1,0:T(8,128)(2,1)S(1)}, u32[]{:S(2)}, u32[]{:S(2)}) %collective-permute-start) | collective-permute-done | bytes 311328 | tf_op jit(solution)/shard_map/ppermute | solution.py:277
  18.3 6.8 %collective-permute-done.2.refs_3_ = bf16[304,512]{1,0:T(8,128)(2,1)S(1)} collective-permute-done((bf16[304,512]{1,0:T(8,128)(2,1)S(1)}, bf16[304,512]{1,0:T(8,128)(2,1)S(1)}, u32[]{:S(2)}, u32[]{:S(2)}) %collective-permute-start.2) | collective-permute-done | bytes 311328 | tf_op jit(solution)/shard_map/ppermute | solution.py:277
  25.2 4.9 %collective-permute-start.3 = (bf16[4,304,256]{2,1,0:T(8,128)(2,1)S(1)}, bf16[4,304,256]{2,1,0:T(8,128)(2,1)S(1)}, u32[]{:S(2)}, u32[]{:S(2)}) collective-permute-start(bf16[4,304,256]{2,1,0:T(8,128)(2,1)S(1)} %pad_maximum_fusion), channel_id=1, source_target_pairs={{0,4},{4,8},{8,12},{12,16},{16,20},{20,24},{24,28},{1,5},{5,9},{9,... | collective-permute-start | bytes 1867784 | tf_op jit(solution)/shard_map/ppermute | solution.py:271
  32.8 4.4 %collective-permute-done.3.refs_4_ = bf16[4,304,256]{2,1,0:T(8,128)(2,1)S(1)} collective-permute-done((bf16[4,304,256]{2,1,0:T(8,128)(2,1)S(1)}, bf16[4,304,256]{2,1,0:T(8,128)(2,1)S(1)}, u32[]{:S(2)}, u32[]{:S(2)}) %collective-permute-start.3) | collective-permute-done | bytes 622624 | tf_op jit(solution)/shard_map/ppermute | solution.py:271
  37.2 2.7 %shard_map.89 = (bf16[4,288,256]{2,1,0:T(8,128)(2,1)S(1)}, bf16[4,288,256]{2,1,0:T(8,128)(2,1)S(1)}, f32[4,288,256]{2,1,0:T(8,128)S(1)}) custom-call(bf16[304,512]{1,0:T(8,128)(2,1)S(1)} %get-tuple-element.67.refs_0_, bf16[304,512]{1,0:T(8,128)(2,1)S(1)} %collective-permute-done.refs_1_, bf16[304,512]{1,0:T(8,128)(2,1)S(1)} %collective-permute-done.1.refs_2_, ...), custom_call_target="tpu_custom_call" | custom-call | flops 6000000000 | bytes 20000000 | tf_op jit(solution)/shard_map/pallas_call | solution.py:37
  39.9 6.5 %collective-permute-done.5.refs_3_ = bf16[304,512]{1,0:T(8,128)(2,1)S(1)} collective-permute-done((bf16[304,512]{1,0:T(8,128)(2,1)S(1)}, bf16[304,512]{1,0:T(8,128)(2,1)S(1)}, u32[]{:S(2)}, u32[]{:S(2)}) %collective-permute-start.5) | collective-permute-done | bytes 311328 | tf_op jit(solution)/shard_map/ppermute | solution.py:277
  46.4 1.9 %collective-permute-start.7 = (bf16[4,288,256]{2,1,0:T(8,128)(2,1)S(1)}, bf16[4,288,256]{2,1,0:T(8,128)(2,1)S(1)}, u32[]{:S(2)}, u32[]{:S(2)}) collective-permute-start(bf16[4,288,256]{2,1,0:T(8,128)(2,1)S(1)} %get-tuple-element.77), channel_id=1, source_target_pairs={{4,0},{8,4},{12,8},{16,12},{20,16},{24,20},{28,24},{5,1},{9,5},{13... | collective-permute-start | bytes 1769480 | tf_op jit(solution)/shard_map/ppermute | solution.py:271
  48.5 3.6 %collective-permute-start.8 = (bf16[4,304,256]{2,1,0:T(8,128)(2,1)S(1)}, bf16[4,304,256]{2,1,0:T(8,128)(2,1)S(1)}, u32[]{:S(2)}, u32[]{:S(2)}) collective-permute-start(bf16[4,304,256]{2,1,0:T(8,128)(2,1)S(1)} %pad_maximum_fusion.1), channel_id=1, source_target_pairs={{0,4},{4,8},{8,12},{12,16},{16,20},{20,24},{24,28},{1,5},{5,9},{9,... | collective-permute-start | bytes 1867784 | tf_op jit(solution)/shard_map/ppermute | solution.py:271
  54.9 3.1 %collective-permute-done.7.refs_2_ = bf16[4,288,256]{2,1,0:T(8,128)(2,1)S(1)} collective-permute-done((bf16[4,288,256]{2,1,0:T(8,128)(2,1)S(1)}, bf16[4,288,256]{2,1,0:T(8,128)(2,1)S(1)}, u32[]{:S(2)}, u32[]{:S(2)}) %collective-permute-start.7) | collective-permute-done | bytes 589856 | tf_op jit(solution)/shard_map/ppermute | solution.py:271
  59.9 2.7 %shard_map.91 = (bf16[4,288,256]{2,1,0:T(8,128)(2,1)S(1)}, bf16[4,288,256]{2,1,0:T(8,128)(2,1)S(1)}, f32[4,288,256]{2,1,0:T(8,128)S(1)}) custom-call(bf16[288,512]{1,0:T(8,128)(2,1)S(1)} %get-tuple-element.78.refs_0_.refs_2_, bf16[304,512]{1,0:T(8,128)(2,1)S(1)} %get-tuple-element.79.refs_1_, bf16[304,512]{1,0:T(8,128)(2,1)S(1)} %collective-permute-done.4.refs_2_, ...), custom_call_target="tpu_custom_call" | custom-call | flops 6000000000 | bytes 20000000 | tf_op jit(solution)/shard_map/pallas_call | solution.py:37
  64.6 2.9 %collective-permute-start.12 = (bf16[4,288,256]{2,1,0:T(8,128)(2,1)S(1)}, bf16[4,288,256]{2,1,0:T(8,128)(2,1)S(1)}, u32[]{:S(2)}, u32[]{:S(2)}) collective-permute-start(bf16[4,288,256]{2,1,0:T(8,128)(2,1)S(1)} %get-tuple-element.89), channel_id=1, source_target_pairs={{4,0},{8,4},{12,8},{16,12},{20,16},{24,20},{28,24},{5,1},{9,5},{13... | collective-permute-start | bytes 1769480 | tf_op jit(solution)/shard_map/ppermute | solution.py:271
  67.6 3.3 %collective-permute-start.13 = (bf16[4,208,256]{2,1,0:T(8,128)(2,1)S(1)}, bf16[4,208,256]{2,1,0:T(8,128)(2,1)S(1)}, u32[]{:S(2)}, u32[]{:S(2)}) collective-permute-start(bf16[4,208,256]{2,1,0:T(8,128)(2,1)S(1)} %pad_maximum_fusion.2), channel_id=1, source_target_pairs={{0,4},{4,8},{8,12},{12,16},{16,20},{20,24},{24,28},{1,5},{5,9},{9,... | collective-permute-start | bytes 1277960 | tf_op jit(solution)/shard_map/ppermute | solution.py:271
  71.0 5.6 %collective-permute-done.12.refs_2_ = bf16[4,288,256]{2,1,0:T(8,128)(2,1)S(1)} collective-permute-done((bf16[4,288,256]{2,1,0:T(8,128)(2,1)S(1)}, bf16[4,288,256]{2,1,0:T(8,128)(2,1)S(1)}, u32[]{:S(2)}, u32[]{:S(2)}) %collective-permute-start.12) | collective-permute-done | bytes 589856 | tf_op jit(solution)/shard_map/ppermute | solution.py:271
  78.3 1.9 %shard_map.93 = (bf16[4,192,256]{2,1,0:T(8,128)(2,1)S(1)}, bf16[4,192,256]{2,1,0:T(8,128)(2,1)S(1)}, f32[4,192,256]{2,1,0:T(8,128)S(1)}) custom-call(bf16[288,512]{1,0:T(8,128)(2,1)S(1)} %get-tuple-element.90.refs_0_.refs_2_, bf16[208,512]{1,0:T(8,128)(2,1)S(1)} %get-tuple-element.91.refs_1_, bf16[208,512]{1,0:T(8,128)(2,1)S(1)} %collective-permute-done.9.refs_2_, ...), custom_call_target="tpu_custom_call" | custom-call | flops 6000000000 | bytes 20000000 | tf_op jit(solution)/shard_map/pallas_call | solution.py:37
  81.4 1.9 %collective-permute-start.14 = (bf16[4,192,256]{2,1,0:T(8,128)(2,1)S(1)}, bf16[4,192,256]{2,1,0:T(8,128)(2,1)S(1)}, u32[]{:S(2)}, u32[]{:S(2)}) collective-permute-start(bf16[4,192,256]{2,1,0:T(8,128)(2,1)S(1)} %get-tuple-element.97), channel_id=1, source_target_pairs={{4,0},{8,4},{12,8},{16,12},{20,16},{24,20},{28,24},{5,1},{9,5},{13... | collective-permute-start | bytes 1179656 | tf_op jit(solution)/shard_map/ppermute | solution.py:271
  83.3 3.2 %shard_map.95.refs_6_ = bf16[1536,512]{1,0:T(8,128)(2,1)S(1)} custom-call(bf16[288,512]{1,0:T(8,128)(2,1)S(1)} %get-tuple-element.90.refs_0_.refs_2_, s32[1536,128]{1,0:T(8,128)S(1)} %get-tuple-element.57.refs_1_.refs_0_, bf16[288,512]{1,0:T(8,128)(2,1)S(1)} %get-tuple-element.78.refs_0_.refs_2_, bf16[288,512]{1,0:T(8,128)(2,1)S(1)} %collective-permute-done.21.refs_3_, ...), custom_call_target="tpu_custom_call" | custom-call | flops 6000000000 | bytes 20000000 | tf_op jit(solution)/shard_map/pallas_call | solution.py:37
  86.6 4.2 %collective-permute-done.14.refs_2_ = bf16[4,192,256]{2,1,0:T(8,128)(2,1)S(1)} collective-permute-done((bf16[4,192,256]{2,1,0:T(8,128)(2,1)S(1)}, bf16[4,192,256]{2,1,0:T(8,128)(2,1)S(1)}, u32[]{:S(2)}, u32[]{:S(2)}) %collective-permute-start.14) | collective-permute-done | bytes 393248 | tf_op jit(solution)/shard_map/ppermute | solution.py:271
  93.6 3.3 %shard_map.96.refs_5_ = bf16[1536,512]{1,0:T(8,128)(2,1)S(1)} custom-call(bf16[192,512]{1,0:T(8,128)(2,1)S(1)} %get-tuple-element.98.refs_0_.refs_1_, s32[1536,128]{1,0:T(8,128)S(1)} %get-tuple-element.57.refs_1_.refs_0_, bf16[288,512]{1,0:T(8,128)(2,1)S(1)} %get-tuple-element.90.refs_0_.refs_2_, bf16[288,512]{1,0:T(8,128)(2,1)S(1)} %collective-permute-done.18.refs_3_, ...), custom_call_target="tpu_custom_call" | custom-call | flops 6000000000 | bytes 20000000 | tf_op jit(solution)/shard_map/pallas_call | solution.py:37
  97.9 2.6 %collective-permute-done.16.refs_3_ = bf16[192,512]{1,0:T(8,128)(2,1)S(1)} collective-permute-done((bf16[192,512]{1,0:T(8,128)(2,1)S(1)}, bf16[192,512]{1,0:T(8,128)(2,1)S(1)}, u32[]{:S(2)}, u32[]{:S(2)}) %collective-permute-start.16) | collective-permute-done | bytes 196640 | tf_op jit(solution)/shard_map/ppermute | solution.py:277
  101.3 3.4 %shard_map.97 = (bf16[1536,128]{1,0:T(8,128)(2,1)}, bf16[1536,384]{1,0:T(8,128)(2,1)}, f32[8,192]{1,0:T(8,128)}) custom-call(s32[1536,128]{1,0:T(8,128)S(1)} %get-tuple-element.57.refs_1_.refs_0_, bf16[192,512]{1,0:T(8,128)(2,1)S(1)} %get-tuple-element.98.refs_0_.refs_1_, bf16[192,512]{1,0:T(8,128)(2,1)S(1)} %collective-permute-done.15.refs_2_, ...), custom_call_target="tpu_custom_call" | custom-call | flops 6000000000 | bytes 20000000 | tf_op jit(solution)/shard_map/pallas_call | solution.py:37
  (66 shorter events, 25.8 us)
Async XLA Ops:
  9.1 8.3 %collective-permute-start = (bf16[304,512]{1,0:T(8,128)(2,1)S(1)}, bf16[304,512]{1,0:T(8,128)(2,1)S(1)}, u32[]{:S(2)}, u32[]{:S(2)}) collective-permute-start(bf16[304,512]{1,0:T(8,128)(2,1)S(1)} %get-tuple-element.62), channel_id=1, source_target_pairs={{0,1},{1,0},{2,3},{3,2},{4,5},{5,4},{6,7},{7,6},{8,9},{9,8},{10,11... | collective-permute-start | bytes 933896 | tf_op jit(solution)/shard_map/ppermute | solution.py:277
  10.4 7.9 %collective-permute-start.1 = (bf16[304,512]{1,0:T(8,128)(2,1)S(1)}, bf16[304,512]{1,0:T(8,128)(2,1)S(1)}, u32[]{:S(2)}, u32[]{:S(2)}) collective-permute-start(bf16[304,512]{1,0:T(8,128)(2,1)S(1)} %get-tuple-element.63), channel_id=1, source_target_pairs={{0,2},{1,3},{2,0},{3,1},{4,6},{5,7},{6,4},{7,5},{8,10},{9,11},{10,... | collective-permute-start | bytes 933896 | tf_op jit(solution)/shard_map/ppermute | solution.py:277
  11.6 13.4 %collective-permute-start.2 = (bf16[304,512]{1,0:T(8,128)(2,1)S(1)}, bf16[304,512]{1,0:T(8,128)(2,1)S(1)}, u32[]{:S(2)}, u32[]{:S(2)}) collective-permute-start(bf16[304,512]{1,0:T(8,128)(2,1)S(1)} %get-tuple-element.64), channel_id=1, source_target_pairs={{0,3},{1,2},{2,1},{3,0},{4,7},{5,6},{6,5},{7,4},{8,11},{9,10},{10,... | collective-permute-start | bytes 933896 | tf_op jit(solution)/shard_map/ppermute | solution.py:277
  25.2 12.0 %collective-permute-start.3 = (bf16[4,304,256]{2,1,0:T(8,128)(2,1)S(1)}, bf16[4,304,256]{2,1,0:T(8,128)(2,1)S(1)}, u32[]{:S(2)}, u32[]{:S(2)}) collective-permute-start(bf16[4,304,256]{2,1,0:T(8,128)(2,1)S(1)} %pad_maximum_fusion), channel_id=1, source_target_pairs={{0,4},{4,8},{8,12},{12,16},{16,20},{20,24},{24,28},{1,5},{5,9},{9,... | collective-permute-start | bytes 1867784 | tf_op jit(solution)/shard_map/ppermute | solution.py:271
  30.1 9.8 %collective-permute-start.4 = (bf16[304,512]{1,0:T(8,128)(2,1)S(1)}, bf16[304,512]{1,0:T(8,128)(2,1)S(1)}, u32[]{:S(2)}, u32[]{:S(2)}) collective-permute-start(bf16[304,512]{1,0:T(8,128)(2,1)S(1)} %get-tuple-element.73), channel_id=1, source_target_pairs={{0,1},{1,0},{2,3},{3,2},{4,5},{5,4},{6,7},{7,6},{8,9},{9,8},{10,11... | collective-permute-start | bytes 933896 | tf_op jit(solution)/shard_map/ppermute | solution.py:277
  31.1 15.3 %collective-permute-start.5 = (bf16[304,512]{1,0:T(8,128)(2,1)S(1)}, bf16[304,512]{1,0:T(8,128)(2,1)S(1)}, u32[]{:S(2)}, u32[]{:S(2)}) collective-permute-start(bf16[304,512]{1,0:T(8,128)(2,1)S(1)} %get-tuple-element.74), channel_id=1, source_target_pairs={{0,2},{1,3},{2,0},{3,1},{4,6},{5,7},{6,4},{7,5},{8,10},{9,11},{10,... | collective-permute-start | bytes 933896 | tf_op jit(solution)/shard_map/ppermute | solution.py:277
  31.6 14.8 %collective-permute-start.6 = (bf16[304,512]{1,0:T(8,128)(2,1)S(1)}, bf16[304,512]{1,0:T(8,128)(2,1)S(1)}, u32[]{:S(2)}, u32[]{:S(2)}) collective-permute-start(bf16[304,512]{1,0:T(8,128)(2,1)S(1)} %get-tuple-element.75), channel_id=1, source_target_pairs={{0,3},{1,2},{2,1},{3,0},{4,7},{5,6},{6,5},{7,4},{8,11},{9,10},{10,... | collective-permute-start | bytes 933896 | tf_op jit(solution)/shard_map/ppermute | solution.py:277
  46.4 11.5 %collective-permute-start.7 = (bf16[4,288,256]{2,1,0:T(8,128)(2,1)S(1)}, bf16[4,288,256]{2,1,0:T(8,128)(2,1)S(1)}, u32[]{:S(2)}, u32[]{:S(2)}) collective-permute-start(bf16[4,288,256]{2,1,0:T(8,128)(2,1)S(1)} %get-tuple-element.77), channel_id=1, source_target_pairs={{4,0},{8,4},{12,8},{16,12},{20,16},{24,20},{28,24},{5,1},{9,5},{13... | collective-permute-start | bytes 1769480 | tf_op jit(solution)/shard_map/ppermute | solution.py:271
  48.5 10.8 %collective-permute-start.8 = (bf16[4,304,256]{2,1,0:T(8,128)(2,1)S(1)}, bf16[4,304,256]{2,1,0:T(8,128)(2,1)S(1)}, u32[]{:S(2)}, u32[]{:S(2)}) collective-permute-start(bf16[4,304,256]{2,1,0:T(8,128)(2,1)S(1)} %pad_maximum_fusion.1), channel_id=1, source_target_pairs={{0,4},{4,8},{8,12},{12,16},{16,20},{20,24},{24,28},{1,5},{5,9},{9,... | collective-permute-start | bytes 1867784 | tf_op jit(solution)/shard_map/ppermute | solution.py:271
  52.1 10.4 %collective-permute-start.9 = (bf16[208,512]{1,0:T(8,128)(2,1)S(1)}, bf16[208,512]{1,0:T(8,128)(2,1)S(1)}, u32[]{:S(2)}, u32[]{:S(2)}) collective-permute-start(bf16[208,512]{1,0:T(8,128)(2,1)S(1)} %get-tuple-element.85), channel_id=1, source_target_pairs={{0,1},{1,0},{2,3},{3,2},{4,5},{5,4},{6,7},{7,6},{8,9},{9,8},{10,11... | collective-permute-start | bytes 638984 | tf_op jit(solution)/shard_map/ppermute | solution.py:277
  52.7 11.8 %collective-permute-start.10 = (bf16[208,512]{1,0:T(8,128)(2,1)S(1)}, bf16[208,512]{1,0:T(8,128)(2,1)S(1)}, u32[]{:S(2)}, u32[]{:S(2)}) collective-permute-start(bf16[208,512]{1,0:T(8,128)(2,1)S(1)} %get-tuple-element.86), channel_id=1, source_target_pairs={{0,2},{1,3},{2,0},{3,1},{4,6},{5,7},{6,4},{7,5},{8,10},{9,11},{10,... | collective-permute-start | bytes 638984 | tf_op jit(solution)/shard_map/ppermute | solution.py:277
  54.0 10.6 %collective-permute-start.11 = (bf16[208,512]{1,0:T(8,128)(2,1)S(1)}, bf16[208,512]{1,0:T(8,128)(2,1)S(1)}, u32[]{:S(2)}, u32[]{:S(2)}) collective-permute-start(bf16[208,512]{1,0:T(8,128)(2,1)S(1)} %get-tuple-element.87), channel_id=1, source_target_pairs={{0,3},{1,2},{2,1},{3,0},{4,7},{5,6},{6,5},{7,4},{8,11},{9,10},{10,... | collective-permute-start | bytes 638984 | tf_op jit(solution)/shard_map/ppermute | solution.py:277
  58.1 22.1 %collective-permute-start.21 = (bf16[288,512]{1,0:T(8,128)(2,1)S(1)}, bf16[288,512]{1,0:T(8,128)(2,1)S(1)}, u32[]{:S(2)}, u32[]{:S(2)}) collective-permute-start(bf16[288,512]{1,0:T(8,128)(2,1)S(1)} %get-tuple-element.105), channel_id=1, source_target_pairs={{0,1},{1,0},{2,3},{3,2},{4,5},{5,4},{6,7},{7,6},{8,9},{9,8},{10,11... | collective-permute-start | bytes 884744 | tf_op jit(solution)/shard_map/ppermute | solution.py:277
  59.3 22.1 %collective-permute-start.22 = (bf16[288,512]{1,0:T(8,128)(2,1)S(1)}, bf16[288,512]{1,0:T(8,128)(2,1)S(1)}, u32[]{:S(2)}, u32[]{:S(2)}) collective-permute-start(bf16[288,512]{1,0:T(8,128)(2,1)S(1)} %get-tuple-element.106), channel_id=1, source_target_pairs={{0,2},{1,3},{2,0},{3,1},{4,6},{5,7},{6,4},{7,5},{8,10},{9,11},{10,... | collective-permute-start | bytes 884744 | tf_op jit(solution)/shard_map/ppermute | solution.py:277
  62.6 20.7 %collective-permute-start.23 = (bf16[288,512]{1,0:T(8,128)(2,1)S(1)}, bf16[288,512]{1,0:T(8,128)(2,1)S(1)}, u32[]{:S(2)}, u32[]{:S(2)}) collective-permute-start(bf16[288,512]{1,0:T(8,128)(2,1)S(1)} %get-tuple-element.107), channel_id=1, source_target_pairs={{0,3},{1,2},{2,1},{3,0},{4,7},{5,6},{6,5},{7,4},{8,11},{9,10},{10,... | collective-permute-start | bytes 884744 | tf_op jit(solution)/shard_map/ppermute | solution.py:277
  64.6 12.0 %collective-permute-start.12 = (bf16[4,288,256]{2,1,0:T(8,128)(2,1)S(1)}, bf16[4,288,256]{2,1,0:T(8,128)(2,1)S(1)}, u32[]{:S(2)}, u32[]{:S(2)}) collective-permute-start(bf16[4,288,256]{2,1,0:T(8,128)(2,1)S(1)} %get-tuple-element.89), channel_id=1, source_target_pairs={{4,0},{8,4},{12,8},{16,12},{20,16},{24,20},{28,24},{5,1},{9,5},{13... | collective-permute-start | bytes 1769480 | tf_op jit(solution)/shard_map/ppermute | solution.py:271
  67.6 10.0 %collective-permute-start.13 = (bf16[4,208,256]{2,1,0:T(8,128)(2,1)S(1)}, bf16[4,208,256]{2,1,0:T(8,128)(2,1)S(1)}, u32[]{:S(2)}, u32[]{:S(2)}) collective-permute-start(bf16[4,208,256]{2,1,0:T(8,128)(2,1)S(1)} %pad_maximum_fusion.2), channel_id=1, source_target_pairs={{0,4},{4,8},{8,12},{12,16},{16,20},{20,24},{24,28},{1,5},{5,9},{9,... | collective-permute-start | bytes 1277960 | tf_op jit(solution)/shard_map/ppermute | solution.py:271
  76.7 16.0 %collective-permute-start.18 = (bf16[288,512]{1,0:T(8,128)(2,1)S(1)}, bf16[288,512]{1,0:T(8,128)(2,1)S(1)}, u32[]{:S(2)}, u32[]{:S(2)}) collective-permute-start(bf16[288,512]{1,0:T(8,128)(2,1)S(1)} %get-tuple-element.102), channel_id=1, source_target_pairs={{0,1},{1,0},{2,3},{3,2},{4,5},{5,4},{6,7},{7,6},{8,9},{9,8},{10,11... | collective-permute-start | bytes 884744 | tf_op jit(solution)/shard_map/ppermute | solution.py:277
  77.6 16.0 %collective-permute-start.19 = (bf16[288,512]{1,0:T(8,128)(2,1)S(1)}, bf16[288,512]{1,0:T(8,128)(2,1)S(1)}, u32[]{:S(2)}, u32[]{:S(2)}) collective-permute-start(bf16[288,512]{1,0:T(8,128)(2,1)S(1)} %get-tuple-element.103), channel_id=1, source_target_pairs={{0,2},{1,3},{2,0},{3,1},{4,6},{5,7},{6,4},{7,5},{8,10},{9,11},{10,... | collective-permute-start | bytes 884744 | tf_op jit(solution)/shard_map/ppermute | solution.py:277
  80.2 13.4 %collective-permute-start.20 = (bf16[288,512]{1,0:T(8,128)(2,1)S(1)}, bf16[288,512]{1,0:T(8,128)(2,1)S(1)}, u32[]{:S(2)}, u32[]{:S(2)}) collective-permute-start(bf16[288,512]{1,0:T(8,128)(2,1)S(1)} %get-tuple-element.104), channel_id=1, source_target_pairs={{0,3},{1,2},{2,1},{3,0},{4,7},{5,6},{6,5},{7,4},{8,11},{9,10},{10,... | collective-permute-start | bytes 884744 | tf_op jit(solution)/shard_map/ppermute | solution.py:277
  81.4 9.4 %collective-permute-start.14 = (bf16[4,192,256]{2,1,0:T(8,128)(2,1)S(1)}, bf16[4,192,256]{2,1,0:T(8,128)(2,1)S(1)}, u32[]{:S(2)}, u32[]{:S(2)}) collective-permute-start(bf16[4,192,256]{2,1,0:T(8,128)(2,1)S(1)} %get-tuple-element.97), channel_id=1, source_target_pairs={{4,0},{8,4},{12,8},{16,12},{20,16},{24,20},{28,24},{5,1},{9,5},{13... | collective-permute-start | bytes 1179656 | tf_op jit(solution)/shard_map/ppermute | solution.py:271
  90.9 7.0 %collective-permute-start.15 = (bf16[192,512]{1,0:T(8,128)(2,1)S(1)}, bf16[192,512]{1,0:T(8,128)(2,1)S(1)}, u32[]{:S(2)}, u32[]{:S(2)}) collective-permute-start(bf16[192,512]{1,0:T(8,128)(2,1)S(1)} %get-tuple-element.99), channel_id=1, source_target_pairs={{0,1},{1,0},{2,3},{3,2},{4,5},{5,4},{6,7},{7,6},{8,9},{9,8},{10,11... | collective-permute-start | bytes 589832 | tf_op jit(solution)/shard_map/ppermute | solution.py:277
  91.8 8.8 %collective-permute-start.16 = (bf16[192,512]{1,0:T(8,128)(2,1)S(1)}, bf16[192,512]{1,0:T(8,128)(2,1)S(1)}, u32[]{:S(2)}, u32[]{:S(2)}) collective-permute-start(bf16[192,512]{1,0:T(8,128)(2,1)S(1)} %get-tuple-element.100), channel_id=1, source_target_pairs={{0,2},{1,3},{2,0},{3,1},{4,6},{5,7},{6,4},{7,5},{8,10},{9,11},{10,... | collective-permute-start | bytes 589832 | tf_op jit(solution)/shard_map/ppermute | solution.py:277
  92.7 8.6 %collective-permute-start.17 = (bf16[192,512]{1,0:T(8,128)(2,1)S(1)}, bf16[192,512]{1,0:T(8,128)(2,1)S(1)}, u32[]{:S(2)}, u32[]{:S(2)}) collective-permute-start(bf16[192,512]{1,0:T(8,128)(2,1)S(1)} %get-tuple-element.101), channel_id=1, source_target_pairs={{0,3},{1,2},{2,1},{3,0},{4,7},{5,6},{6,5},{7,4},{8,11},{9,10},{10,... | collective-permute-start | bytes 589832 | tf_op jit(solution)/shard_map/ppermute | solution.py:277
  (8 other events, 20.5 us)

commit v3 on v2

--- a/solution.py
+++ b/solution.py
@@ -13,10 +13,14 @@
 DOC_ROWS = 16
 DOC_LANES = 64
 PARTS = (6, 6, 4)
+COSTS = (6, 6, 6, 6)
+PREPARE_BYTES = 60 * 1024 * 1024
 KERNEL_BYTES = 20 * 1024 * 1024
 TOGETHER = 2
 
 VMEM = pl.BlockSpec(memory_space=pltpu.VMEM)
+ANY = pl.BlockSpec(memory_space=pl.ANY)
+HBM = pl.BlockSpec(memory_space=pltpu.HBM)
 
 
 def head_chunks(heads):
@@ -27,7 +31,7 @@
     return [(a, b - a) for a, b in zip(edges[:-1], edges[1:]) if b > a]
 
 
-def call(kernel, out_shape, *operands, after=(), scratch=(), in_specs=None, pairs=0):
+def call(kernel, out_shape, *operands, after=(), scratch=(), in_specs=None, pairs=0, cost=0.0, limit=0):
     waits = len(after)
     specs = in_specs or [VMEM] * len(operands)
 
@@ -37,11 +41,13 @@
     return pl.pallas_call(
         body,
         out_shape=out_shape,
-        in_specs=[pl.BlockSpec(memory_space=pl.ANY)] * waits + specs,
+        in_specs=[ANY] * waits + specs,
         out_specs=jax.tree.map(lambda _: VMEM, out_shape),
         scratch_shapes=list(scratch),
-        cost_estimate=pl.CostEstimate(flops=6 * 10**9, bytes_accessed=20 * 10**6, transcendentals=0),
-        compiler_params=pltpu.CompilerParams(vmem_limit_bytes=KERNEL_BYTES + 40 * pairs),
+        cost_estimate=pl.CostEstimate(
+            flops=int(cost * 1e9), bytes_accessed=int(cost * 3.4e6), transcendentals=0
+        ),
+        compiler_params=pltpu.CompilerParams(vmem_limit_bytes=limit or KERNEL_BYTES + 40 * pairs),
     )(*after, *operands)
 
 
@@ -86,14 +92,24 @@
     return 1.0 / (1.0 + jnp.exp(-x))
 
 
-def prepare_kernel(heads_ref, slots_ref, logits_ref, doc_lengths_ref, proj_ref, cot_ref,
-                   flat_ref, column_ref, docs_ref, rows_ref):
+def prepare_kernel(first, count, owned, groups, heads_in, slots_in, logits_in, doc_lengths_ref,
+                   proj_in, cot_in, *refs):
+    flat_ref, column_ref, docs_ref, rows_ref = refs[:4]
+    out_refs = refs[4 : groups + 4]
+    heads_ref, slots_ref, logits_ref, proj_ref, cot_ref, hot_ref, sems = refs[groups + 4 :]
+    pairs = [
+        (heads_in, heads_ref), (slots_in, slots_ref), (logits_in, logits_ref),
+        (cot_in, cot_ref), (proj_in, proj_ref),
+    ]
+    copies = [pltpu.make_async_copy(a, b, sems.at[i]) for i, (a, b) in enumerate(pairs)]
+    for copy in copies:
+        copy.start()
+    for copy in copies[:3]:
+        copy.wait()
     top, tokens = heads_ref.shape
     routes = tokens * top
     width = proj_ref.shape[1]
     gate = route_column(sigmoid(logits_ref[...]))
-    rows_ref[:, :width] = proj_ref[...]
-    rows_ref[:, width:] = (cot_ref[...].astype(jnp.float32) * gate).astype(jnp.bfloat16)
     slots = route_column((heads_ref[...] * CAP + slots_ref[...]).astype(jnp.float32))
     slots = jnp.broadcast_to(slots, (routes, 128))
     column_ref[...] = slots.astype(jnp.int32)
@@ -106,6 +122,11 @@
         end = end + doc_lengths_ref[i]
         docs = docs + jnp.where(position >= end, 1.0, 0.0)
     docs_ref[...] = docs
+    copies[3].wait()
+    rows_ref[:, width:] = (cot_ref[...].astype(jnp.float32) * gate).astype(jnp.bfloat16)
+    copies[4].wait()
+    rows_ref[:, :width] = proj_ref[...]
+    dispatch_kernel(first, count, owned, groups, flat_ref, docs_ref, rows_ref, *out_refs, hot_ref)
 
 
 def dispatch_kernel(first, count, owned, groups, flat_ref, docs_ref, rows_ref, *refs):
@@ -290,76 +311,107 @@
     shape = jax.ShapeDtypeStruct
     logits = gate_logits.T
     cot_rows = cotangent.reshape(routes, head_size)
-    flat, columns, documents, rows_in = call(
-        prepare_kernel,
+    chunks = head_chunks(owned)
+    last = len(chunks) - 1
+
+    def sent_shapes(count):
+        return [shape((count * CAP + DOC_ROWS, width + head_size), bf16)] * groups
+
+    def hot_scratch(count):
+        return pltpu.VMEM((groups * count * CAP, routes), bf16)
+
+    flat, columns, documents, rows_in, *sent = call(
+        partial(prepare_kernel, *chunks[0], owned, groups),
         [
             shape((8, routes), jnp.int32),
             shape((routes, 128), jnp.int32),
             shape((8, routes), f32),
             shape((routes, width + head_size), bf16),
-        ],
+        ]
+        + sent_shapes(chunks[0][1]),
         routed_heads.T,
         slot_index.T,
         logits,
         doc_lengths,
         projections.reshape(routes, width),
         cot_rows,
-        in_specs=[VMEM] * 3 + [pl.BlockSpec(memory_space=pltpu.SMEM)] + [VMEM] * 2,
-    )
-
-    chunks = head_chunks(owned)
-    last = len(chunks) - 1
-    blocks_out = []
-    for first, count in chunks:
-        rows = count * CAP
+        in_specs=[ANY] * 3 + [pl.BlockSpec(memory_space=pltpu.SMEM)] + [ANY] * 2,
+        scratch=[
+            pltpu.VMEM((top, tokens), jnp.int32),
+            pltpu.VMEM((top, tokens), jnp.int32),
+            pltpu.VMEM((top, tokens), f32),
+            pltpu.VMEM((routes, width), bf16),
+            pltpu.VMEM((routes, head_size), bf16),
+            hot_scratch(chunks[0][1]),
+            pltpu.SemaphoreType.DMA((5,)),
+        ],
+        limit=PREPARE_BYTES,
+        cost=COSTS[0],
+    )
+    blocks_out = [sent]
+    for first, count in chunks[1:]:
         sent = call(
             partial(dispatch_kernel, first, count, owned, groups),
-            [shape((rows + DOC_ROWS, width + head_size), bf16)] * groups,
+            sent_shapes(count),
             flat,
             documents,
             rows_in,
-            scratch=[pltpu.VMEM((groups * rows, routes), bf16)],
+            scratch=[hot_scratch(count)],
+            cost=COSTS[0],
         )
         blocks_out.append(sent)
-    received = [exchanged(sent) for sent in blocks_out]
-
-    homes, fars = [], []
+    received = []
+    for i, sent in enumerate(blocks_out):
+        with jax.named_scope(f"send_out_{i}"):
+            received.append(exchanged(sent))
+
+    homes, fars, returned = [], [], []
     for i, ((first, count), blocks) in enumerate(zip(chunks, received)):
         rows = count * CAP
         if i > 0:
-            *blocks, fars[-1] = lax.optimization_barrier((*blocks, fars[-1]))
+            *blocks, _ = lax.optimization_barrier((*blocks, fars[-1]))
         else:
             waits = [sent[0] for sent in blocks_out[1:]]
             blocks = lax.optimization_barrier((*blocks, *waits))[: len(blocks)]
-        before = shifted(jnp.stack([b[:, head_size : 3 * head_size] for b in blocks]), "seq", 1)
+        with jax.named_scope(f"send_next_{i}"):
+            before = shifted(jnp.stack([b[:, head_size : 3 * head_size] for b in blocks]), "seq", 1)
         if i > 0:
-            homes.append(finish_chunk(fars[-1]))
+            homes.append(finish_chunk(incoming))
+            with jax.named_scope(f"send_home_{i - 1}"):
+                returned.append(exchanged(homes[-1]))
         pair = (groups, rows, 2 * head_size)
         near, far, own = call(
             partial(attention_kernel, count, groups),
             [shape(pair, bf16), shape(pair, bf16), shape(pair, f32)],
             *blocks,
             before,
-            after=homes[-1][:1] if homes else (),
+            after=[homes[-1][0]] if homes else (),
             scratch=[pltpu.VMEM((groups * CAP, 2 * groups * CAP), f32)],
             pairs=2 * (groups * CAP) ** 2,
+            cost=COSTS[1],
         )
         fars.append(far)
 
-        def finish_chunk(far, near=near, own=own, rows=rows):
+        with jax.named_scope(f"send_back_{i}"):
+            incoming = shifted(far, "seq", -1)
+
+        def finish_chunk(incoming, near=near, own=own, rows=rows):
             return call(
                 partial(combine_kernel, groups),
                 [shape((rows, 4 * head_size), bf16)] * groups,
                 near,
                 own,
-                shifted(far, "seq", -1),
+                incoming,
+                cost=COSTS[2],
             )
 
-    homes.append(finish_chunk(fars[-1]))
+    homes.append(finish_chunk(incoming))
+    with jax.named_scope(f"send_home_{last}"):
+        returned.append(exchanged(homes[-1]))
     total = []
     for i, ((first, count), home) in enumerate(zip(chunks, homes)):
         rows = count * CAP
-        operands = [columns, *exchanged(home), *total]
+        operands = [columns, *returned[i], *total]
         scratch = [pltpu.VMEM((routes, groups * rows), bf16)]
         if i < last:
             total = [
@@ -369,6 +421,7 @@
                     *operands,
                     after=[homes[i + 1][0]],
                     scratch=scratch,
+                    cost=COSTS[3],
                 )
             ]
     head_outputs, projection_grads, gate_grads = call(

time: 106 us -> 101 us (0.953)
  waiting for transfers between devices: 39.5 us -> 33.1 us
  Pallas kernels: 24.4 us -> 26.5 us
  local copies, waits for them, and re-layouts: 5.14 us -> 3.17 us
  starting transfers between devices: 34.5 us -> 36.2 us
    ppermute x18, waiting for transfers between devices: 21.5 us -> 15.9 us  [exchanged(): lax.ppermute(blocks[d], 'head', [(i, i ^ d) for i in range(groups)])]
    pallas_call x13 -> x12, Pallas kernels: 24.4 us -> 26.5 us  [call(): pl.pallas_call(body, out_shape=out_shape, in_specs=[ANY] * waits + specs,...]
    unnamed x16, local copies, waits for them, and re-layouts: 5.01 us -> 3.04 us
  transfers between devices with their start and end apart: 24 -> 24, of which waited for: 13 -> 11; matrix products, arithmetic and copies ran while one was open for 0% -> 0% of each run, Pallas kernels for 17% -> 18%
where the time goes in v3:
time: 101 us; the launch traced here: 100 us
  starting transfers between devices  36.2 us (36%)
  waiting for transfers between devices  33.1 us (33%)
  Pallas kernels  26.5 us (26%)
  local copies, waits for them, and re-layouts  3.17 us (3%)
    pallas_call x12, Pallas kernels, call(): pl.pallas_call(body, out_shape=out_shape, in_specs=[ANY] * waits + specs,...  26.5 us
    ppermute x6, starting transfers between devices, shifted(): return lax.ppermute(block, axis, route)  19.2 us
    ppermute x6, waiting for transfers between devices, shifted(): return lax.ppermute(block, axis, route)  17.2 us
    ppermute x18, starting transfers between devices, exchanged(): lax.ppermute(blocks[d], 'head', [(i, i ^ d) for i in range(groups)])  17 us
    ppermute x18, waiting for transfers between devices, exchanged(): lax.ppermute(blocks[d], 'head', [(i, i ^ d) for i in range(groups)])  15.9 us
    unnamed x16, local copies, waits for them, and re-layouts  3.04 us
  transfers between devices with their start and end apart: 24, of which 11 were waited for; matrix products, arithmetic and copies ran while one was open for 0% of the time, Pallas kernels for 18%

profile of v3, /device:TPU:9, one launch (start us, length us, event | category | flops | bytes accessed | tf_op | source)
XLA Modules:
  0.0 100.1 jit_solution(1126155295449737780)
XLA Ops:
  0.6 5.5 %shard_map.85 = (s32[8,1536]{1,0:T(8,128)}, s32[1536,128]{1,0:T(8,128)}, f32[8,1536]{1,0:T(8,128)}, bf16[1536,512]{1,0:T(8,128)(2,1)}, bf16[304,512]{1,0:T(8,128...) custom-call(s32[8,192]{1,0:T(8,128)} %bitcast.39, s32[8,192]{1,0:T(8,128)} %bitcast.40, ...), custom_call_target="tpu_custom_call" | custom-call | flops 6000000000 | bytes 20400000 | tf_op jit(solution)/shard_map/pallas_call | solution.py:41
  6.2 1.3 %collective-permute-start = (bf16[304,512]{1,0:T(8,128)(2,1)}, bf16[304,512]{1,0:T(8,128)(2,1)S(1)}, u32[]{:S(2)}, u32[]{:S(2)}) collective-permute-start(bf16[304,512]{1,0:T(8,128)(2,1)} %get-tuple-element.57), channel_id=1, source_target_pairs={{0,1},{1,0},{2,3},{3,2},{4,5},{5,4},{6,7},{7,6},{8,9},{9,8},{10,11... | collective-permute-start | bytes 933896 | tf_op jit(solution)/shard_map/send_out_0/ppermute | solution.py:298
  8.9 1.4 %copy-done.4 = bf16[1536,512]{1,0:T(8,128)(2,1)S(1)} copy-done((bf16[1536,512]{1,0:T(8,128)(2,1)S(1)}, bf16[1536,512]{1,0:T(8,128)(2,1)}, u32[]{:S(2)}) %copy-start.4) | copy-done | bytes 1572888
  11.9 1.4 %shard_map.87 = (bf16[208,512]{1,0:T(8,128)(2,1)S(1)}, bf16[208,512]{1,0:T(8,128)(2,1)S(1)}, bf16[208,512]{1,0:T(8,128)(2,1)S(1)}, bf16[208,512]{1,0:T(8,128)(2,1)S(1)}) custom-call(s32[8,1536]{1,0:T(8,128)S(1)} %copy-done.6, f32[8,1536]{1,0:T(8,128)S(1)} %copy-done.7, bf16[1536,512]{1,0:T(8,128)(2,1)S(1)} %copy-done.4), custom_call_target="tpu_custom_call" | custom-call | flops 6000000000 | bytes 20400000 | tf_op jit(solution)/shard_map/pallas_call | solution.py:41
  13.3 2.0 %shard_map.86 = (bf16[304,512]{1,0:T(8,128)(2,1)S(1)}, bf16[304,512]{1,0:T(8,128)(2,1)S(1)}, bf16[304,512]{1,0:T(8,128)(2,1)S(1)}, bf16[304,512]{1,0:T(8,128)(2,1)S(1)}) custom-call(s32[8,1536]{1,0:T(8,128)S(1)} %copy-done.6, f32[8,1536]{1,0:T(8,128)S(1)} %copy-done.7, bf16[1536,512]{1,0:T(8,128)(2,1)S(1)} %copy-done.5), custom_call_target="tpu_custom_call" | custom-call | flops 6000000000 | bytes 20400000 | tf_op jit(solution)/shard_map/pallas_call | solution.py:41
  15.6 6.8 %collective-permute-done.2.refs_3_ = bf16[304,512]{1,0:T(8,128)(2,1)S(1)} collective-permute-done((bf16[304,512]{1,0:T(8,128)(2,1)}, bf16[304,512]{1,0:T(8,128)(2,1)S(1)}, u32[]{:S(2)}, u32[]{:S(2)}) %collective-permute-start.2) | collective-permute-done | bytes 311328 | tf_op jit(solution)/shard_map/send_out_0/ppermute | solution.py:298
  22.5 4.8 %collective-permute-start.3 = (bf16[4,304,256]{2,1,0:T(8,128)(2,1)S(1)}, bf16[4,304,256]{2,1,0:T(8,128)(2,1)S(1)}, u32[]{:S(2)}, u32[]{:S(2)}) collective-permute-start(bf16[4,304,256]{2,1,0:T(8,128)(2,1)S(1)} %pad_maximum_fusion), channel_id=1, source_target_pairs={{0,4},{4,8},{8,12},{12,16},{16,20},{20,24},{24,28},{1,5},{5,9},{9,... | collective-permute-start | bytes 1867784 | tf_op jit(solution)/shard_map/send_next_0/ppermute | solution.py:292
  30.1 4.4 %collective-permute-done.3.refs_4_ = bf16[4,304,256]{2,1,0:T(8,128)(2,1)S(1)} collective-permute-done((bf16[4,304,256]{2,1,0:T(8,128)(2,1)S(1)}, bf16[4,304,256]{2,1,0:T(8,128)(2,1)S(1)}, u32[]{:S(2)}, u32[]{:S(2)}) %collective-permute-start.3) | collective-permute-done | bytes 622624 | tf_op jit(solution)/shard_map/send_next_0/ppermute | solution.py:292
  34.5 2.7 %shard_map.88 = (bf16[4,288,256]{2,1,0:T(8,128)(2,1)S(1)}, bf16[4,288,256]{2,1,0:T(8,128)(2,1)S(1)}, f32[4,288,256]{2,1,0:T(8,128)S(1)}) custom-call(bf16[304,512]{1,0:T(8,128)(2,1)S(1)} %copy-done.2, bf16[304,512]{1,0:T(8,128)(2,1)S(1)} %collective-permute-done.refs_1_, bf16[304,512]{1,0:T(8,128)(2,1)S(1)} %collective-permute-done.1.refs_2_, ...), custom_call_target="tpu_custom_call" | custom-call | flops 6000000000 | bytes 20400000 | tf_op jit(solution)/shard_map/pallas_call | solution.py:41
  37.2 3.2 %collective-permute-start.4 = (bf16[4,288,256]{2,1,0:T(8,128)(2,1)S(1)}, bf16[4,288,256]{2,1,0:T(8,128)(2,1)S(1)}, u32[]{:S(2)}, u32[]{:S(2)}) collective-permute-start(bf16[4,288,256]{2,1,0:T(8,128)(2,1)S(1)} %get-tuple-element.71), channel_id=1, source_target_pairs={{4,0},{8,4},{12,8},{16,12},{20,16},{24,20},{28,24},{5,1},{9,5},{13... | collective-permute-start | bytes 1769480 | tf_op jit(solution)/shard_map/send_back_0/ppermute | solution.py:292
  40.4 3.3 %collective-permute-done.6.refs_3_ = bf16[304,512]{1,0:T(8,128)(2,1)S(1)} collective-permute-done((bf16[304,512]{1,0:T(8,128)(2,1)S(1)}, bf16[304,512]{1,0:T(8,128)(2,1)S(1)}, u32[]{:S(2)}, u32[]{:S(2)}) %collective-permute-start.6) | collective-permute-done | bytes 311328 | tf_op jit(solution)/shard_map/send_out_1/ppermute | solution.py:298
  43.9 3.1 %collective-permute-start.8 = (bf16[4,304,256]{2,1,0:T(8,128)(2,1)S(1)}, bf16[4,304,256]{2,1,0:T(8,128)(2,1)S(1)}, u32[]{:S(2)}, u32[]{:S(2)}) collective-permute-start(bf16[4,304,256]{2,1,0:T(8,128)(2,1)S(1)} %pad_maximum_fusion.1), channel_id=1, source_target_pairs={{0,4},{4,8},{8,12},{12,16},{16,20},{20,24},{24,28},{1,5},{5,9},{9,... | collective-permute-start | bytes 1867784 | tf_op jit(solution)/shard_map/send_next_1/ppermute | solution.py:292
  50.9 3.0 %collective-permute-done.8.refs_5_ = bf16[4,304,256]{2,1,0:T(8,128)(2,1)S(1)} collective-permute-done((bf16[4,304,256]{2,1,0:T(8,128)(2,1)S(1)}, bf16[4,304,256]{2,1,0:T(8,128)(2,1)S(1)}, u32[]{:S(2)}, u32[]{:S(2)}) %collective-permute-start.8) | collective-permute-done | bytes 622624 | tf_op jit(solution)/shard_map/send_next_1/ppermute | solution.py:292
  55.0 2.7 %shard_map.90 = (bf16[4,288,256]{2,1,0:T(8,128)(2,1)S(1)}, bf16[4,288,256]{2,1,0:T(8,128)(2,1)S(1)}, f32[4,288,256]{2,1,0:T(8,128)S(1)}) custom-call(bf16[288,512]{1,0:T(8,128)(2,1)S(1)} %get-tuple-element.72.refs_0_.refs_2_, bf16[304,512]{1,0:T(8,128)(2,1)S(1)} %get-tuple-element.76.refs_1_, bf16[304,512]{1,0:T(8,128)(2,1)S(1)} %collective-permute-done.5.refs_2_, ...), custom_call_target="tpu_custom_call" | custom-call | flops 6000000000 | bytes 20400000 | tf_op jit(solution)/shard_map/pallas_call | solution.py:41
  59.9 2.8 %collective-permute-start.9 = (bf16[4,288,256]{2,1,0:T(8,128)(2,1)S(1)}, bf16[4,288,256]{2,1,0:T(8,128)(2,1)S(1)}, u32[]{:S(2)}, u32[]{:S(2)}) collective-permute-start(bf16[4,288,256]{2,1,0:T(8,128)(2,1)S(1)} %get-tuple-element.82), channel_id=1, source_target_pairs={{4,0},{8,4},{12,8},{16,12},{20,16},{24,20},{28,24},{5,1},{9,5},{13... | collective-permute-start | bytes 1769480 | tf_op jit(solution)/shard_map/send_back_1/ppermute | solution.py:292
  62.8 3.1 %collective-permute-start.13 = (bf16[4,208,256]{2,1,0:T(8,128)(2,1)S(1)}, bf16[4,208,256]{2,1,0:T(8,128)(2,1)S(1)}, u32[]{:S(2)}, u32[]{:S(2)}) collective-permute-start(bf16[4,208,256]{2,1,0:T(8,128)(2,1)S(1)} %pad_maximum_fusion.2), channel_id=1, source_target_pairs={{0,4},{4,8},{8,12},{12,16},{16,20},{20,24},{24,28},{1,5},{5,9},{9,... | collective-permute-start | bytes 1277960 | tf_op jit(solution)/shard_map/send_next_2/ppermute | solution.py:292
  66.0 5.8 %collective-permute-done.9.refs_2_ = bf16[4,288,256]{2,1,0:T(8,128)(2,1)S(1)} collective-permute-done((bf16[4,288,256]{2,1,0:T(8,128)(2,1)S(1)}, bf16[4,288,256]{2,1,0:T(8,128)(2,1)S(1)}, u32[]{:S(2)}, u32[]{:S(2)}) %collective-permute-start.9) | collective-permute-done | bytes 589856 | tf_op jit(solution)/shard_map/send_back_1/ppermute | solution.py:292
  73.4 1.9 %shard_map.92 = (bf16[4,192,256]{2,1,0:T(8,128)(2,1)S(1)}, bf16[4,192,256]{2,1,0:T(8,128)(2,1)S(1)}, f32[4,192,256]{2,1,0:T(8,128)S(1)}) custom-call(bf16[288,512]{1,0:T(8,128)(2,1)S(1)} %get-tuple-element.83.refs_0_.refs_2_, bf16[208,512]{1,0:T(8,128)(2,1)S(1)} %get-tuple-element.87.refs_1_, bf16[208,512]{1,0:T(8,128)(2,1)S(1)} %collective-permute-done.10.refs_2_, ...), custom_call_target="tpu_custom_call" | custom-call | flops 6000000000 | bytes 20400000 | tf_op jit(solution)/shard_map/pallas_call | solution.py:41
  76.6 2.1 %collective-permute-start.14 = (bf16[4,192,256]{2,1,0:T(8,128)(2,1)S(1)}, bf16[4,192,256]{2,1,0:T(8,128)(2,1)S(1)}, u32[]{:S(2)}, u32[]{:S(2)}) collective-permute-start(bf16[4,192,256]{2,1,0:T(8,128)(2,1)S(1)} %get-tuple-element.93), channel_id=1, source_target_pairs={{4,0},{8,4},{12,8},{16,12},{20,16},{24,20},{28,24},{5,1},{9,5},{13... | collective-permute-start | bytes 1179656 | tf_op jit(solution)/shard_map/send_back_2/ppermute | solution.py:292
  78.7 3.2 %shard_map.94.refs_6_ = bf16[1536,512]{1,0:T(8,128)(2,1)S(1)} custom-call(bf16[288,512]{1,0:T(8,128)(2,1)S(1)} %get-tuple-element.83.refs_0_.refs_2_, s32[1536,128]{1,0:T(8,128)S(1)} %copy-done, bf16[288,512]{1,0:T(8,128)(2,1)S(1)} %get-tuple-element.72.refs_0_.refs_2_, bf16[288,512]{1,0:T(8,128)(2,1)S(1)} %collective-permute-done.21.refs_3_, ...), custom_call_target="tpu_custom_call" | custom-call | flops 6000000000 | bytes 20400000 | tf_op jit(solution)/shard_map/pallas_call | solution.py:41
  82.0 4.0 %collective-permute-done.14.refs_2_ = bf16[4,192,256]{2,1,0:T(8,128)(2,1)S(1)} collective-permute-done((bf16[4,192,256]{2,1,0:T(8,128)(2,1)S(1)}, bf16[4,192,256]{2,1,0:T(8,128)(2,1)S(1)}, u32[]{:S(2)}, u32[]{:S(2)}) %collective-permute-start.14) | collective-permute-done | bytes 393248 | tf_op jit(solution)/shard_map/send_back_2/ppermute | solution.py:292
  88.8 3.3 %shard_map.95.refs_5_ = bf16[1536,512]{1,0:T(8,128)(2,1)S(1)} custom-call(bf16[192,512]{1,0:T(8,128)(2,1)S(1)} %get-tuple-element.94.refs_0_.refs_1_, s32[1536,128]{1,0:T(8,128)S(1)} %copy-done, bf16[288,512]{1,0:T(8,128)(2,1)S(1)} %get-tuple-element.83.refs_0_.refs_2_, bf16[288,512]{1,0:T(8,128)(2,1)S(1)} %collective-permute-done.18.refs_3_, ...), custom_call_target="tpu_custom_call" | custom-call | flops 6000000000 | bytes 20400000 | tf_op jit(solution)/shard_map/pallas_call | solution.py:41
  93.0 2.8 %collective-permute-done.16.refs_3_ = bf16[192,512]{1,0:T(8,128)(2,1)S(1)} collective-permute-done((bf16[192,512]{1,0:T(8,128)(2,1)S(1)}, bf16[192,512]{1,0:T(8,128)(2,1)S(1)}, u32[]{:S(2)}, u32[]{:S(2)}) %collective-permute-start.16) | collective-permute-done | bytes 196640 | tf_op jit(solution)/shard_map/send_home_2/ppermute | solution.py:298
  96.7 3.4 %shard_map.96 = (bf16[1536,128]{1,0:T(8,128)(2,1)}, bf16[1536,384]{1,0:T(8,128)(2,1)}, f32[8,192]{1,0:T(8,128)}) custom-call(s32[1536,128]{1,0:T(8,128)S(1)} %copy-done, bf16[192,512]{1,0:T(8,128)(2,1)S(1)} %get-tuple-element.94.refs_0_.refs_1_, bf16[192,512]{1,0:T(8,128)(2,1)S(1)} %collective-permute-done.15.refs_2_, ...), custom_call_target="tpu_custom_call" | custom-call | tf_op jit(solution)/shard_map/pallas_call | solution.py:41
  (65 shorter events, 21.1 us)
Async XLA Ops:
  6.2 9.2 %collective-permute-start = (bf16[304,512]{1,0:T(8,128)(2,1)}, bf16[304,512]{1,0:T(8,128)(2,1)S(1)}, u32[]{:S(2)}, u32[]{:S(2)}) collective-permute-start(bf16[304,512]{1,0:T(8,128)(2,1)} %get-tuple-element.57), channel_id=1, source_target_pairs={{0,1},{1,0},{2,3},{3,2},{4,5},{5,4},{6,7},{7,6},{8,9},{9,8},{10,11... | collective-permute-start | bytes 933896 | tf_op jit(solution)/shard_map/send_out_0/ppermute | solution.py:298
  7.5 8.1 %collective-permute-start.1 = (bf16[304,512]{1,0:T(8,128)(2,1)}, bf16[304,512]{1,0:T(8,128)(2,1)S(1)}, u32[]{:S(2)}, u32[]{:S(2)}) collective-permute-start(bf16[304,512]{1,0:T(8,128)(2,1)} %get-tuple-element.58), channel_id=1, source_target_pairs={{0,2},{1,3},{2,0},{3,1},{4,6},{5,7},{6,4},{7,5},{8,10},{9,11},{10,... | collective-permute-start | bytes 933896 | tf_op jit(solution)/shard_map/send_out_0/ppermute | solution.py:298
  8.7 13.7 %collective-permute-start.2 = (bf16[304,512]{1,0:T(8,128)(2,1)}, bf16[304,512]{1,0:T(8,128)(2,1)S(1)}, u32[]{:S(2)}, u32[]{:S(2)}) collective-permute-start(bf16[304,512]{1,0:T(8,128)(2,1)} %get-tuple-element.59), channel_id=1, source_target_pairs={{0,3},{1,2},{2,1},{3,0},{4,7},{5,6},{6,5},{7,4},{8,11},{9,10},{10,... | collective-permute-start | bytes 933896 | tf_op jit(solution)/shard_map/send_out_0/ppermute | solution.py:298
  22.5 12.0 %collective-permute-start.3 = (bf16[4,304,256]{2,1,0:T(8,128)(2,1)S(1)}, bf16[4,304,256]{2,1,0:T(8,128)(2,1)S(1)}, u32[]{:S(2)}, u32[]{:S(2)}) collective-permute-start(bf16[4,304,256]{2,1,0:T(8,128)(2,1)S(1)} %pad_maximum_fusion), channel_id=1, source_target_pairs={{0,4},{4,8},{8,12},{12,16},{16,20},{20,24},{24,28},{1,5},{5,9},{9,... | collective-permute-start | bytes 1867784 | tf_op jit(solution)/shard_map/send_next_0/ppermute | solution.py:292
  27.4 13.1 %collective-permute-start.5 = (bf16[304,512]{1,0:T(8,128)(2,1)S(1)}, bf16[304,512]{1,0:T(8,128)(2,1)S(1)}, u32[]{:S(2)}, u32[]{:S(2)}) collective-permute-start(bf16[304,512]{1,0:T(8,128)(2,1)S(1)} %get-tuple-element.73), channel_id=1, source_target_pairs={{0,1},{1,0},{2,3},{3,2},{4,5},{5,4},{6,7},{7,6},{8,9},{9,8},{10,11... | collective-permute-start | bytes 933896 | tf_op jit(solution)/shard_map/send_out_1/ppermute | solution.py:298
  28.4 15.3 %collective-permute-start.6 = (bf16[304,512]{1,0:T(8,128)(2,1)S(1)}, bf16[304,512]{1,0:T(8,128)(2,1)S(1)}, u32[]{:S(2)}, u32[]{:S(2)}) collective-permute-start(bf16[304,512]{1,0:T(8,128)(2,1)S(1)} %get-tuple-element.74), channel_id=1, source_target_pairs={{0,2},{1,3},{2,0},{3,1},{4,6},{5,7},{6,4},{7,5},{8,10},{9,11},{10,... | collective-permute-start | bytes 933896 | tf_op jit(solution)/shard_map/send_out_1/ppermute | solution.py:298
  28.9 14.8 %collective-permute-start.7 = (bf16[304,512]{1,0:T(8,128)(2,1)S(1)}, bf16[304,512]{1,0:T(8,128)(2,1)S(1)}, u32[]{:S(2)}, u32[]{:S(2)}) collective-permute-start(bf16[304,512]{1,0:T(8,128)(2,1)S(1)} %get-tuple-element.75), channel_id=1, source_target_pairs={{0,3},{1,2},{2,1},{3,0},{4,7},{5,6},{6,5},{7,4},{8,11},{9,10},{10,... | collective-permute-start | bytes 933896 | tf_op jit(solution)/shard_map/send_out_1/ppermute | solution.py:298
  37.2 12.5 %collective-permute-start.4 = (bf16[4,288,256]{2,1,0:T(8,128)(2,1)S(1)}, bf16[4,288,256]{2,1,0:T(8,128)(2,1)S(1)}, u32[]{:S(2)}, u32[]{:S(2)}) collective-permute-start(bf16[4,288,256]{2,1,0:T(8,128)(2,1)S(1)} %get-tuple-element.71), channel_id=1, source_target_pairs={{4,0},{8,4},{12,8},{16,12},{20,16},{24,20},{28,24},{5,1},{9,5},{13... | collective-permute-start | bytes 1769480 | tf_op jit(solution)/shard_map/send_back_0/ppermute | solution.py:292
  43.9 10.1 %collective-permute-start.8 = (bf16[4,304,256]{2,1,0:T(8,128)(2,1)S(1)}, bf16[4,304,256]{2,1,0:T(8,128)(2,1)S(1)}, u32[]{:S(2)}, u32[]{:S(2)}) collective-permute-start(bf16[4,304,256]{2,1,0:T(8,128)(2,1)S(1)} %pad_maximum_fusion.1), channel_id=1, source_target_pairs={{0,4},{4,8},{8,12},{12,16},{16,20},{20,24},{24,28},{1,5},{5,9},{9,... | collective-permute-start | bytes 1867784 | tf_op jit(solution)/shard_map/send_next_1/ppermute | solution.py:292
  47.0 10.7 %collective-permute-start.10 = (bf16[208,512]{1,0:T(8,128)(2,1)S(1)}, bf16[208,512]{1,0:T(8,128)(2,1)S(1)}, u32[]{:S(2)}, u32[]{:S(2)}) collective-permute-start(bf16[208,512]{1,0:T(8,128)(2,1)S(1)} %get-tuple-element.84), channel_id=1, source_target_pairs={{0,1},{1,0},{2,3},{3,2},{4,5},{5,4},{6,7},{7,6},{8,9},{9,8},{10,11... | collective-permute-start | bytes 638984 | tf_op jit(solution)/shard_map/send_out_2/ppermute | solution.py:298
  48.1 11.8 %collective-permute-start.11 = (bf16[208,512]{1,0:T(8,128)(2,1)S(1)}, bf16[208,512]{1,0:T(8,128)(2,1)S(1)}, u32[]{:S(2)}, u32[]{:S(2)}) collective-permute-start(bf16[208,512]{1,0:T(8,128)(2,1)S(1)} %get-tuple-element.85), channel_id=1, source_target_pairs={{0,2},{1,3},{2,0},{3,1},{4,6},{5,7},{6,4},{7,5},{8,10},{9,11},{10,... | collective-permute-start | bytes 638984 | tf_op jit(solution)/shard_map/send_out_2/ppermute | solution.py:298
  49.3 13.4 %collective-permute-start.12 = (bf16[208,512]{1,0:T(8,128)(2,1)S(1)}, bf16[208,512]{1,0:T(8,128)(2,1)S(1)}, u32[]{:S(2)}, u32[]{:S(2)}) collective-permute-start(bf16[208,512]{1,0:T(8,128)(2,1)S(1)} %get-tuple-element.86), channel_id=1, source_target_pairs={{0,3},{1,2},{2,1},{3,0},{4,7},{5,6},{6,5},{7,4},{8,11},{9,10},{10,... | collective-permute-start | bytes 638984 | tf_op jit(solution)/shard_map/send_out_2/ppermute | solution.py:298
  49.8 25.5 %collective-permute-start.21 = (bf16[288,512]{1,0:T(8,128)(2,1)S(1)}, bf16[288,512]{1,0:T(8,128)(2,1)S(1)}, u32[]{:S(2)}, u32[]{:S(2)}) collective-permute-start(bf16[288,512]{1,0:T(8,128)(2,1)S(1)} %get-tuple-element.101), channel_id=1, source_target_pairs={{0,1},{1,0},{2,3},{3,2},{4,5},{5,4},{6,7},{7,6},{8,9},{9,8},{10,11... | collective-permute-start | bytes 884744 | tf_op jit(solution)/shard_map/send_home_0/ppermute | solution.py:298
  54.0 22.6 %collective-permute-start.22 = (bf16[288,512]{1,0:T(8,128)(2,1)S(1)}, bf16[288,512]{1,0:T(8,128)(2,1)S(1)}, u32[]{:S(2)}, u32[]{:S(2)}) collective-permute-start(bf16[288,512]{1,0:T(8,128)(2,1)S(1)} %get-tuple-element.102), channel_id=1, source_target_pairs={{0,2},{1,3},{2,0},{3,1},{4,6},{5,7},{6,4},{7,5},{8,10},{9,11},{10,... | collective-permute-start | bytes 884744 | tf_op jit(solution)/shard_map/send_home_0/ppermute | solution.py:298
  57.7 21.0 %collective-permute-start.23 = (bf16[288,512]{1,0:T(8,128)(2,1)S(1)}, bf16[288,512]{1,0:T(8,128)(2,1)S(1)}, u32[]{:S(2)}, u32[]{:S(2)}) collective-permute-start(bf16[288,512]{1,0:T(8,128)(2,1)S(1)} %get-tuple-element.103), channel_id=1, source_target_pairs={{0,3},{1,2},{2,1},{3,0},{4,7},{5,6},{6,5},{7,4},{8,11},{9,10},{10,... | collective-permute-start | bytes 884744 | tf_op jit(solution)/shard_map/send_home_0/ppermute | solution.py:298
  59.9 11.8 %collective-permute-start.9 = (bf16[4,288,256]{2,1,0:T(8,128)(2,1)S(1)}, bf16[4,288,256]{2,1,0:T(8,128)(2,1)S(1)}, u32[]{:S(2)}, u32[]{:S(2)}) collective-permute-start(bf16[4,288,256]{2,1,0:T(8,128)(2,1)S(1)} %get-tuple-element.82), channel_id=1, source_target_pairs={{4,0},{8,4},{12,8},{16,12},{20,16},{24,20},{28,24},{5,1},{9,5},{13... | collective-permute-start | bytes 1769480 | tf_op jit(solution)/shard_map/send_back_1/ppermute | solution.py:292
  62.8 9.5 %collective-permute-start.13 = (bf16[4,208,256]{2,1,0:T(8,128)(2,1)S(1)}, bf16[4,208,256]{2,1,0:T(8,128)(2,1)S(1)}, u32[]{:S(2)}, u32[]{:S(2)}) collective-permute-start(bf16[4,208,256]{2,1,0:T(8,128)(2,1)S(1)} %pad_maximum_fusion.2), channel_id=1, source_target_pairs={{0,4},{4,8},{8,12},{12,16},{16,20},{20,24},{24,28},{1,5},{5,9},{9,... | collective-permute-start | bytes 1277960 | tf_op jit(solution)/shard_map/send_next_2/ppermute | solution.py:292
  71.9 15.8 %collective-permute-start.18 = (bf16[288,512]{1,0:T(8,128)(2,1)S(1)}, bf16[288,512]{1,0:T(8,128)(2,1)S(1)}, u32[]{:S(2)}, u32[]{:S(2)}) collective-permute-start(bf16[288,512]{1,0:T(8,128)(2,1)S(1)} %get-tuple-element.98), channel_id=1, source_target_pairs={{0,1},{1,0},{2,3},{3,2},{4,5},{5,4},{6,7},{7,6},{8,9},{9,8},{10,11... | collective-permute-start | bytes 884744 | tf_op jit(solution)/shard_map/send_home_1/ppermute | solution.py:298
  72.4 16.4 %collective-permute-start.19 = (bf16[288,512]{1,0:T(8,128)(2,1)S(1)}, bf16[288,512]{1,0:T(8,128)(2,1)S(1)}, u32[]{:S(2)}, u32[]{:S(2)}) collective-permute-start(bf16[288,512]{1,0:T(8,128)(2,1)S(1)} %get-tuple-element.99), channel_id=1, source_target_pairs={{0,2},{1,3},{2,0},{3,1},{4,6},{5,7},{6,4},{7,5},{8,10},{9,11},{10,... | collective-permute-start | bytes 884744 | tf_op jit(solution)/shard_map/send_home_1/ppermute | solution.py:298
  75.3 13.4 %collective-permute-start.20 = (bf16[288,512]{1,0:T(8,128)(2,1)S(1)}, bf16[288,512]{1,0:T(8,128)(2,1)S(1)}, u32[]{:S(2)}, u32[]{:S(2)}) collective-permute-start(bf16[288,512]{1,0:T(8,128)(2,1)S(1)} %get-tuple-element.100), channel_id=1, source_target_pairs={{0,3},{1,2},{2,1},{3,0},{4,7},{5,6},{6,5},{7,4},{8,11},{9,10},{10,... | collective-permute-start | bytes 884744 | tf_op jit(solution)/shard_map/send_home_1/ppermute | solution.py:298
  76.6 9.4 %collective-permute-start.14 = (bf16[4,192,256]{2,1,0:T(8,128)(2,1)S(1)}, bf16[4,192,256]{2,1,0:T(8,128)(2,1)S(1)}, u32[]{:S(2)}, u32[]{:S(2)}) collective-permute-start(bf16[4,192,256]{2,1,0:T(8,128)(2,1)S(1)} %get-tuple-element.93), channel_id=1, source_target_pairs={{4,0},{8,4},{12,8},{16,12},{20,16},{24,20},{28,24},{5,1},{9,5},{13... | collective-permute-start | bytes 1179656 | tf_op jit(solution)/shard_map/send_back_2/ppermute | solution.py:292
  86.0 7.0 %collective-permute-start.15 = (bf16[192,512]{1,0:T(8,128)(2,1)S(1)}, bf16[192,512]{1,0:T(8,128)(2,1)S(1)}, u32[]{:S(2)}, u32[]{:S(2)}) collective-permute-start(bf16[192,512]{1,0:T(8,128)(2,1)S(1)} %get-tuple-element.95), channel_id=1, source_target_pairs={{0,1},{1,0},{2,3},{3,2},{4,5},{5,4},{6,7},{7,6},{8,9},{9,8},{10,11... | collective-permute-start | bytes 589832 | tf_op jit(solution)/shard_map/send_home_2/ppermute | solution.py:298
  86.5 9.2 %collective-permute-start.16 = (bf16[192,512]{1,0:T(8,128)(2,1)S(1)}, bf16[192,512]{1,0:T(8,128)(2,1)S(1)}, u32[]{:S(2)}, u32[]{:S(2)}) collective-permute-start(bf16[192,512]{1,0:T(8,128)(2,1)S(1)} %get-tuple-element.96), channel_id=1, source_target_pairs={{0,2},{1,3},{2,0},{3,1},{4,6},{5,7},{6,4},{7,5},{8,10},{9,11},{10,... | collective-permute-start | bytes 589832 | tf_op jit(solution)/shard_map/send_home_2/ppermute | solution.py:298
  87.7 9.0 %collective-permute-start.17 = (bf16[192,512]{1,0:T(8,128)(2,1)S(1)}, bf16[192,512]{1,0:T(8,128)(2,1)S(1)}, u32[]{:S(2)}, u32[]{:S(2)}) collective-permute-start(bf16[192,512]{1,0:T(8,128)(2,1)S(1)} %get-tuple-element.97), channel_id=1, source_target_pairs={{0,3},{1,2},{2,1},{3,0},{4,7},{5,6},{6,5},{7,4},{8,11},{9,10},{10,... | collective-permute-start | bytes 589832 | tf_op jit(solution)/shard_map/send_home_2/ppermute | solution.py:298
  (8 other events, 34.7 us)

commit v4 on v3

--- a/solution.py
+++ b/solution.py
@@ -16,7 +16,7 @@
 COSTS = (6, 6, 6, 6)
 PREPARE_BYTES = 60 * 1024 * 1024
 KERNEL_BYTES = 20 * 1024 * 1024
-TOGETHER = 2
+TOGETHER = 6
 
 VMEM = pl.BlockSpec(memory_space=pltpu.VMEM)
 ANY = pl.BlockSpec(memory_space=pl.ANY)

time: 101 us -> 100 us (0.990)
  transfers between devices with their start and end apart: 24 -> 24, of which waited for: 11 -> 11; matrix products, arithmetic and copies ran while one was open for 0% -> 0% of each run, Pallas kernels for 18% -> 17%
where the time goes in v4:
time: 100 us; the launch traced here: 99.7 us
  starting transfers between devices  35.9 us (36%)
  waiting for transfers between devices  33.6 us (34%)
  Pallas kernels  25.9 us (26%)
  local copies, waits for them, and re-layouts  3.17 us (3%)
    pallas_call x12, Pallas kernels, call(): pl.pallas_call(body, out_shape=out_shape, in_specs=[ANY] * waits + specs,...  25.9 us
    ppermute x6, starting transfers between devices, shifted(): return lax.ppermute(block, axis, route)  18.9 us
    ppermute x6, waiting for transfers between devices, shifted(): return lax.ppermute(block, axis, route)  17.5 us
    ppermute x18, starting transfers between devices, exchanged(): lax.ppermute(blocks[d], 'head', [(i, i ^ d) for i in range(groups)])  17 us
    ppermute x18, waiting for transfers between devices, exchanged(): lax.ppermute(blocks[d], 'head', [(i, i ^ d) for i in range(groups)])  16.1 us
    unnamed x16, local copies, waits for them, and re-layouts  3.04 us
  transfers between devices with their start and end apart: 24, of which 11 were waited for; matrix products, arithmetic and copies ran while one was open for 0% of the time, Pallas kernels for 17%

profile of v4, /device:TPU:9, one launch (start us, length us, event | category | flops | bytes accessed | tf_op | source)
XLA Modules:
  0.0 99.7 jit_solution(2701609435189313296)
XLA Ops:
  0.6 5.5 %shard_map.85 = (s32[8,1536]{1,0:T(8,128)}, s32[1536,128]{1,0:T(8,128)}, f32[8,1536]{1,0:T(8,128)}, bf16[1536,512]{1,0:T(8,128)(2,1)}, bf16[304,512]{1,0:T(8,128...) custom-call(s32[8,192]{1,0:T(8,128)} %bitcast.39, s32[8,192]{1,0:T(8,128)} %bitcast.40, ...), custom_call_target="tpu_custom_call" | custom-call | flops 6000000000 | bytes 20400000 | tf_op jit(solution)/shard_map/pallas_call | solution.py:41
  6.2 1.3 %collective-permute-start = (bf16[304,512]{1,0:T(8,128)(2,1)}, bf16[304,512]{1,0:T(8,128)(2,1)S(1)}, u32[]{:S(2)}, u32[]{:S(2)}) collective-permute-start(bf16[304,512]{1,0:T(8,128)(2,1)} %get-tuple-element.57), channel_id=1, source_target_pairs={{0,1},{1,0},{2,3},{3,2},{4,5},{5,4},{6,7},{7,6},{8,9},{9,8},{10,11... | collective-permute-start | bytes 933896 | tf_op jit(solution)/shard_map/send_out_0/ppermute | solution.py:298
  8.9 1.4 %copy-done.4 = bf16[1536,512]{1,0:T(8,128)(2,1)S(1)} copy-done((bf16[1536,512]{1,0:T(8,128)(2,1)S(1)}, bf16[1536,512]{1,0:T(8,128)(2,1)}, u32[]{:S(2)}) %copy-start.4) | copy-done | bytes 1572888
  11.9 1.4 %shard_map.87 = (bf16[208,512]{1,0:T(8,128)(2,1)S(1)}, bf16[208,512]{1,0:T(8,128)(2,1)S(1)}, bf16[208,512]{1,0:T(8,128)(2,1)S(1)}, bf16[208,512]{1,0:T(8,128)(2,1)S(1)}) custom-call(s32[8,1536]{1,0:T(8,128)S(1)} %copy-done.6, f32[8,1536]{1,0:T(8,128)S(1)} %copy-done.7, bf16[1536,512]{1,0:T(8,128)(2,1)S(1)} %copy-done.4), custom_call_target="tpu_custom_call" | custom-call | flops 6000000000 | bytes 20400000 | tf_op jit(solution)/shard_map/pallas_call | solution.py:41
  13.3 2.0 %shard_map.86 = (bf16[304,512]{1,0:T(8,128)(2,1)S(1)}, bf16[304,512]{1,0:T(8,128)(2,1)S(1)}, bf16[304,512]{1,0:T(8,128)(2,1)S(1)}, bf16[304,512]{1,0:T(8,128)(2,1)S(1)}) custom-call(s32[8,1536]{1,0:T(8,128)S(1)} %copy-done.6, f32[8,1536]{1,0:T(8,128)S(1)} %copy-done.7, bf16[1536,512]{1,0:T(8,128)(2,1)S(1)} %copy-done.5), custom_call_target="tpu_custom_call" | custom-call | flops 6000000000 | bytes 20400000 | tf_op jit(solution)/shard_map/pallas_call | solution.py:41
  15.6 6.8 %collective-permute-done.2.refs_3_ = bf16[304,512]{1,0:T(8,128)(2,1)S(1)} collective-permute-done((bf16[304,512]{1,0:T(8,128)(2,1)}, bf16[304,512]{1,0:T(8,128)(2,1)S(1)}, u32[]{:S(2)}, u32[]{:S(2)}) %collective-permute-start.2) | collective-permute-done | bytes 311328 | tf_op jit(solution)/shard_map/send_out_0/ppermute | solution.py:298
  22.5 4.8 %collective-permute-start.3 = (bf16[4,304,256]{2,1,0:T(8,128)(2,1)S(1)}, bf16[4,304,256]{2,1,0:T(8,128)(2,1)S(1)}, u32[]{:S(2)}, u32[]{:S(2)}) collective-permute-start(bf16[4,304,256]{2,1,0:T(8,128)(2,1)S(1)} %pad_maximum_fusion), channel_id=1, source_target_pairs={{0,4},{4,8},{8,12},{12,16},{16,20},{20,24},{24,28},{1,5},{5,9},{9,... | collective-permute-start | bytes 1867784 | tf_op jit(solution)/shard_map/send_next_0/ppermute | solution.py:292
  30.1 4.4 %collective-permute-done.3.refs_4_ = bf16[4,304,256]{2,1,0:T(8,128)(2,1)S(1)} collective-permute-done((bf16[4,304,256]{2,1,0:T(8,128)(2,1)S(1)}, bf16[4,304,256]{2,1,0:T(8,128)(2,1)S(1)}, u32[]{:S(2)}, u32[]{:S(2)}) %collective-permute-start.3) | collective-permute-done | bytes 622624 | tf_op jit(solution)/shard_map/send_next_0/ppermute | solution.py:292
  34.5 2.5 %shard_map.88 = (bf16[4,288,256]{2,1,0:T(8,128)(2,1)S(1)}, bf16[4,288,256]{2,1,0:T(8,128)(2,1)S(1)}, f32[4,288,256]{2,1,0:T(8,128)S(1)}) custom-call(bf16[304,512]{1,0:T(8,128)(2,1)S(1)} %copy-done.2, bf16[304,512]{1,0:T(8,128)(2,1)S(1)} %collective-permute-done.refs_1_, bf16[304,512]{1,0:T(8,128)(2,1)S(1)} %collective-permute-done.1.refs_2_, ...), custom_call_target="tpu_custom_call" | custom-call | flops 6000000000 | bytes 20400000 | tf_op jit(solution)/shard_map/pallas_call | solution.py:41
  37.0 3.2 %collective-permute-start.4 = (bf16[4,288,256]{2,1,0:T(8,128)(2,1)S(1)}, bf16[4,288,256]{2,1,0:T(8,128)(2,1)S(1)}, u32[]{:S(2)}, u32[]{:S(2)}) collective-permute-start(bf16[4,288,256]{2,1,0:T(8,128)(2,1)S(1)} %get-tuple-element.71), channel_id=1, source_target_pairs={{4,0},{8,4},{12,8},{16,12},{20,16},{24,20},{28,24},{5,1},{9,5},{13... | collective-permute-start | bytes 1769480 | tf_op jit(solution)/shard_map/send_back_0/ppermute | solution.py:292
  40.2 3.5 %collective-permute-done.6.refs_3_ = bf16[304,512]{1,0:T(8,128)(2,1)S(1)} collective-permute-done((bf16[304,512]{1,0:T(8,128)(2,1)S(1)}, bf16[304,512]{1,0:T(8,128)(2,1)S(1)}, u32[]{:S(2)}, u32[]{:S(2)}) %collective-permute-start.6) | collective-permute-done | bytes 311328 | tf_op jit(solution)/shard_map/send_out_1/ppermute | solution.py:298
  43.9 2.9 %collective-permute-start.8 = (bf16[4,304,256]{2,1,0:T(8,128)(2,1)S(1)}, bf16[4,304,256]{2,1,0:T(8,128)(2,1)S(1)}, u32[]{:S(2)}, u32[]{:S(2)}) collective-permute-start(bf16[4,304,256]{2,1,0:T(8,128)(2,1)S(1)} %pad_maximum_fusion.1), channel_id=1, source_target_pairs={{0,4},{4,8},{8,12},{12,16},{16,20},{20,24},{24,28},{1,5},{5,9},{9,... | collective-permute-start | bytes 1867784 | tf_op jit(solution)/shard_map/send_next_1/ppermute | solution.py:292
  50.7 3.2 %collective-permute-done.8.refs_5_ = bf16[4,304,256]{2,1,0:T(8,128)(2,1)S(1)} collective-permute-done((bf16[4,304,256]{2,1,0:T(8,128)(2,1)S(1)}, bf16[4,304,256]{2,1,0:T(8,128)(2,1)S(1)}, u32[]{:S(2)}, u32[]{:S(2)}) %collective-permute-start.8) | collective-permute-done | bytes 622624 | tf_op jit(solution)/shard_map/send_next_1/ppermute | solution.py:292
  55.0 2.5 %shard_map.90 = (bf16[4,288,256]{2,1,0:T(8,128)(2,1)S(1)}, bf16[4,288,256]{2,1,0:T(8,128)(2,1)S(1)}, f32[4,288,256]{2,1,0:T(8,128)S(1)}) custom-call(bf16[288,512]{1,0:T(8,128)(2,1)S(1)} %get-tuple-element.72.refs_0_.refs_2_, bf16[304,512]{1,0:T(8,128)(2,1)S(1)} %get-tuple-element.76.refs_1_, bf16[304,512]{1,0:T(8,128)(2,1)S(1)} %collective-permute-done.5.refs_2_, ...), custom_call_target="tpu_custom_call" | custom-call | flops 6000000000 | bytes 20400000 | tf_op jit(solution)/shard_map/pallas_call | solution.py:41
  59.7 2.8 %collective-permute-start.9 = (bf16[4,288,256]{2,1,0:T(8,128)(2,1)S(1)}, bf16[4,288,256]{2,1,0:T(8,128)(2,1)S(1)}, u32[]{:S(2)}, u32[]{:S(2)}) collective-permute-start(bf16[4,288,256]{2,1,0:T(8,128)(2,1)S(1)} %get-tuple-element.82), channel_id=1, source_target_pairs={{4,0},{8,4},{12,8},{16,12},{20,16},{24,20},{28,24},{5,1},{9,5},{13... | collective-permute-start | bytes 1769480 | tf_op jit(solution)/shard_map/send_back_1/ppermute | solution.py:292
  62.6 3.3 %collective-permute-start.13 = (bf16[4,208,256]{2,1,0:T(8,128)(2,1)S(1)}, bf16[4,208,256]{2,1,0:T(8,128)(2,1)S(1)}, u32[]{:S(2)}, u32[]{:S(2)}) collective-permute-start(bf16[4,208,256]{2,1,0:T(8,128)(2,1)S(1)} %pad_maximum_fusion.2), channel_id=1, source_target_pairs={{0,4},{4,8},{8,12},{12,16},{16,20},{20,24},{24,28},{1,5},{5,9},{9,... | collective-permute-start | bytes 1277960 | tf_op jit(solution)/shard_map/send_next_2/ppermute | solution.py:292
  65.9 5.6 %collective-permute-done.9.refs_2_ = bf16[4,288,256]{2,1,0:T(8,128)(2,1)S(1)} collective-permute-done((bf16[4,288,256]{2,1,0:T(8,128)(2,1)S(1)}, bf16[4,288,256]{2,1,0:T(8,128)(2,1)S(1)}, u32[]{:S(2)}, u32[]{:S(2)}) %collective-permute-start.9) | collective-permute-done | bytes 589856 | tf_op jit(solution)/shard_map/send_back_1/ppermute | solution.py:292
  73.2 1.7 %shard_map.92 = (bf16[4,192,256]{2,1,0:T(8,128)(2,1)S(1)}, bf16[4,192,256]{2,1,0:T(8,128)(2,1)S(1)}, f32[4,192,256]{2,1,0:T(8,128)S(1)}) custom-call(bf16[288,512]{1,0:T(8,128)(2,1)S(1)} %get-tuple-element.83.refs_0_.refs_2_, bf16[208,512]{1,0:T(8,128)(2,1)S(1)} %get-tuple-element.87.refs_1_, bf16[208,512]{1,0:T(8,128)(2,1)S(1)} %collective-permute-done.10.refs_2_, ...), custom_call_target="tpu_custom_call" | custom-call | flops 6000000000 | bytes 20400000 | tf_op jit(solution)/shard_map/pallas_call | solution.py:41
  76.1 1.9 %collective-permute-start.14 = (bf16[4,192,256]{2,1,0:T(8,128)(2,1)S(1)}, bf16[4,192,256]{2,1,0:T(8,128)(2,1)S(1)}, u32[]{:S(2)}, u32[]{:S(2)}) collective-permute-start(bf16[4,192,256]{2,1,0:T(8,128)(2,1)S(1)} %get-tuple-element.93), channel_id=1, source_target_pairs={{4,0},{8,4},{12,8},{16,12},{20,16},{24,20},{28,24},{5,1},{9,5},{13... | collective-permute-start | bytes 1179656 | tf_op jit(solution)/shard_map/send_back_2/ppermute | solution.py:292
  78.1 3.2 %shard_map.94.refs_6_ = bf16[1536,512]{1,0:T(8,128)(2,1)S(1)} custom-call(bf16[288,512]{1,0:T(8,128)(2,1)S(1)} %get-tuple-element.83.refs_0_.refs_2_, s32[1536,128]{1,0:T(8,128)S(1)} %copy-done, bf16[288,512]{1,0:T(8,128)(2,1)S(1)} %get-tuple-element.72.refs_0_.refs_2_, bf16[288,512]{1,0:T(8,128)(2,1)S(1)} %collective-permute-done.21.refs_3_, ...), custom_call_target="tpu_custom_call" | custom-call | flops 6000000000 | bytes 20400000 | tf_op jit(solution)/shard_map/pallas_call | solution.py:41
  81.3 4.2 %collective-permute-done.14.refs_2_ = bf16[4,192,256]{2,1,0:T(8,128)(2,1)S(1)} collective-permute-done((bf16[4,192,256]{2,1,0:T(8,128)(2,1)S(1)}, bf16[4,192,256]{2,1,0:T(8,128)(2,1)S(1)}, u32[]{:S(2)}, u32[]{:S(2)}) %collective-permute-start.14) | collective-permute-done | bytes 393248 | tf_op jit(solution)/shard_map/send_back_2/ppermute | solution.py:292
  88.3 3.3 %shard_map.95.refs_5_ = bf16[1536,512]{1,0:T(8,128)(2,1)S(1)} custom-call(bf16[192,512]{1,0:T(8,128)(2,1)S(1)} %get-tuple-element.94.refs_0_.refs_1_, s32[1536,128]{1,0:T(8,128)S(1)} %copy-done, bf16[288,512]{1,0:T(8,128)(2,1)S(1)} %get-tuple-element.83.refs_0_.refs_2_, bf16[288,512]{1,0:T(8,128)(2,1)S(1)} %collective-permute-done.18.refs_3_, ...), custom_call_target="tpu_custom_call" | custom-call | flops 6000000000 | bytes 20400000 | tf_op jit(solution)/shard_map/pallas_call | solution.py:41
  92.6 2.7 %collective-permute-done.16.refs_3_ = bf16[192,512]{1,0:T(8,128)(2,1)S(1)} collective-permute-done((bf16[192,512]{1,0:T(8,128)(2,1)S(1)}, bf16[192,512]{1,0:T(8,128)(2,1)S(1)}, u32[]{:S(2)}, u32[]{:S(2)}) %collective-permute-start.16) | collective-permute-done | bytes 196640 | tf_op jit(solution)/shard_map/send_home_2/ppermute | solution.py:298
  96.3 3.4 %shard_map.96 = (bf16[1536,128]{1,0:T(8,128)(2,1)}, bf16[1536,384]{1,0:T(8,128)(2,1)}, f32[8,192]{1,0:T(8,128)}) custom-call(s32[1536,128]{1,0:T(8,128)S(1)} %copy-done, bf16[192,512]{1,0:T(8,128)(2,1)S(1)} %get-tuple-element.94.refs_0_.refs_1_, bf16[192,512]{1,0:T(8,128)(2,1)S(1)} %collective-permute-done.15.refs_2_, ...), custom_call_target="tpu_custom_call" | custom-call | tf_op jit(solution)/shard_map/pallas_call | solution.py:41
  (65 shorter events, 21.2 us)
Async XLA Ops:
  6.2 9.2 %collective-permute-start = (bf16[304,512]{1,0:T(8,128)(2,1)}, bf16[304,512]{1,0:T(8,128)(2,1)S(1)}, u32[]{:S(2)}, u32[]{:S(2)}) collective-permute-start(bf16[304,512]{1,0:T(8,128)(2,1)} %get-tuple-element.57), channel_id=1, source_target_pairs={{0,1},{1,0},{2,3},{3,2},{4,5},{5,4},{6,7},{7,6},{8,9},{9,8},{10,11... | collective-permute-start | bytes 933896 | tf_op jit(solution)/shard_map/send_out_0/ppermute | solution.py:298
  7.5 8.1 %collective-permute-start.1 = (bf16[304,512]{1,0:T(8,128)(2,1)}, bf16[304,512]{1,0:T(8,128)(2,1)S(1)}, u32[]{:S(2)}, u32[]{:S(2)}) collective-permute-start(bf16[304,512]{1,0:T(8,128)(2,1)} %get-tuple-element.58), channel_id=1, source_target_pairs={{0,2},{1,3},{2,0},{3,1},{4,6},{5,7},{6,4},{7,5},{8,10},{9,11},{10,... | collective-permute-start | bytes 933896 | tf_op jit(solution)/shard_map/send_out_0/ppermute | solution.py:298
  8.7 13.7 %collective-permute-start.2 = (bf16[304,512]{1,0:T(8,128)(2,1)}, bf16[304,512]{1,0:T(8,128)(2,1)S(1)}, u32[]{:S(2)}, u32[]{:S(2)}) collective-permute-start(bf16[304,512]{1,0:T(8,128)(2,1)} %get-tuple-element.59), channel_id=1, source_target_pairs={{0,3},{1,2},{2,1},{3,0},{4,7},{5,6},{6,5},{7,4},{8,11},{9,10},{10,... | collective-permute-start | bytes 933896 | tf_op jit(solution)/shard_map/send_out_0/ppermute | solution.py:298
  22.5 12.0 %collective-permute-start.3 = (bf16[4,304,256]{2,1,0:T(8,128)(2,1)S(1)}, bf16[4,304,256]{2,1,0:T(8,128)(2,1)S(1)}, u32[]{:S(2)}, u32[]{:S(2)}) collective-permute-start(bf16[4,304,256]{2,1,0:T(8,128)(2,1)S(1)} %pad_maximum_fusion), channel_id=1, source_target_pairs={{0,4},{4,8},{8,12},{12,16},{16,20},{20,24},{24,28},{1,5},{5,9},{9,... | collective-permute-start | bytes 1867784 | tf_op jit(solution)/shard_map/send_next_0/ppermute | solution.py:292
  27.4 12.9 %collective-permute-start.5 = (bf16[304,512]{1,0:T(8,128)(2,1)S(1)}, bf16[304,512]{1,0:T(8,128)(2,1)S(1)}, u32[]{:S(2)}, u32[]{:S(2)}) collective-permute-start(bf16[304,512]{1,0:T(8,128)(2,1)S(1)} %get-tuple-element.73), channel_id=1, source_target_pairs={{0,1},{1,0},{2,3},{3,2},{4,5},{5,4},{6,7},{7,6},{8,9},{9,8},{10,11... | collective-permute-start | bytes 933896 | tf_op jit(solution)/shard_map/send_out_1/ppermute | solution.py:298
  28.4 15.3 %collective-permute-start.6 = (bf16[304,512]{1,0:T(8,128)(2,1)S(1)}, bf16[304,512]{1,0:T(8,128)(2,1)S(1)}, u32[]{:S(2)}, u32[]{:S(2)}) collective-permute-start(bf16[304,512]{1,0:T(8,128)(2,1)S(1)} %get-tuple-element.74), channel_id=1, source_target_pairs={{0,2},{1,3},{2,0},{3,1},{4,6},{5,7},{6,4},{7,5},{8,10},{9,11},{10,... | collective-permute-start | bytes 933896 | tf_op jit(solution)/shard_map/send_out_1/ppermute | solution.py:298
  28.9 14.8 %collective-permute-start.7 = (bf16[304,512]{1,0:T(8,128)(2,1)S(1)}, bf16[304,512]{1,0:T(8,128)(2,1)S(1)}, u32[]{:S(2)}, u32[]{:S(2)}) collective-permute-start(bf16[304,512]{1,0:T(8,128)(2,1)S(1)} %get-tuple-element.75), channel_id=1, source_target_pairs={{0,3},{1,2},{2,1},{3,0},{4,7},{5,6},{6,5},{7,4},{8,11},{9,10},{10,... | collective-permute-start | bytes 933896 | tf_op jit(solution)/shard_map/send_out_1/ppermute | solution.py:298
  37.0 12.5 %collective-permute-start.4 = (bf16[4,288,256]{2,1,0:T(8,128)(2,1)S(1)}, bf16[4,288,256]{2,1,0:T(8,128)(2,1)S(1)}, u32[]{:S(2)}, u32[]{:S(2)}) collective-permute-start(bf16[4,288,256]{2,1,0:T(8,128)(2,1)S(1)} %get-tuple-element.71), channel_id=1, source_target_pairs={{4,0},{8,4},{12,8},{16,12},{20,16},{24,20},{28,24},{5,1},{9,5},{13... | collective-permute-start | bytes 1769480 | tf_op jit(solution)/shard_map/send_back_0/ppermute | solution.py:292
  43.9 10.1 %collective-permute-start.8 = (bf16[4,304,256]{2,1,0:T(8,128)(2,1)S(1)}, bf16[4,304,256]{2,1,0:T(8,128)(2,1)S(1)}, u32[]{:S(2)}, u32[]{:S(2)}) collective-permute-start(bf16[4,304,256]{2,1,0:T(8,128)(2,1)S(1)} %pad_maximum_fusion.1), channel_id=1, source_target_pairs={{0,4},{4,8},{8,12},{12,16},{16,20},{20,24},{24,28},{1,5},{5,9},{9,... | collective-permute-start | bytes 1867784 | tf_op jit(solution)/shard_map/send_next_1/ppermute | solution.py:292
  46.8 10.7 %collective-permute-start.10 = (bf16[208,512]{1,0:T(8,128)(2,1)S(1)}, bf16[208,512]{1,0:T(8,128)(2,1)S(1)}, u32[]{:S(2)}, u32[]{:S(2)}) collective-permute-start(bf16[208,512]{1,0:T(8,128)(2,1)S(1)} %get-tuple-element.84), channel_id=1, source_target_pairs={{0,1},{1,0},{2,3},{3,2},{4,5},{5,4},{6,7},{7,6},{8,9},{9,8},{10,11... | collective-permute-start | bytes 638984 | tf_op jit(solution)/shard_map/send_out_2/ppermute | solution.py:298
  47.9 11.8 %collective-permute-start.11 = (bf16[208,512]{1,0:T(8,128)(2,1)S(1)}, bf16[208,512]{1,0:T(8,128)(2,1)S(1)}, u32[]{:S(2)}, u32[]{:S(2)}) collective-permute-start(bf16[208,512]{1,0:T(8,128)(2,1)S(1)} %get-tuple-element.85), channel_id=1, source_target_pairs={{0,2},{1,3},{2,0},{3,1},{4,6},{5,7},{6,4},{7,5},{8,10},{9,11},{10,... | collective-permute-start | bytes 638984 | tf_op jit(solution)/shard_map/send_out_2/ppermute | solution.py:298
  49.1 13.4 %collective-permute-start.12 = (bf16[208,512]{1,0:T(8,128)(2,1)S(1)}, bf16[208,512]{1,0:T(8,128)(2,1)S(1)}, u32[]{:S(2)}, u32[]{:S(2)}) collective-permute-start(bf16[208,512]{1,0:T(8,128)(2,1)S(1)} %get-tuple-element.86), channel_id=1, source_target_pairs={{0,3},{1,2},{2,1},{3,0},{4,7},{5,6},{6,5},{7,4},{8,11},{9,10},{10,... | collective-permute-start | bytes 638984 | tf_op jit(solution)/shard_map/send_out_2/ppermute | solution.py:298
  49.7 25.2 %collective-permute-start.21 = (bf16[288,512]{1,0:T(8,128)(2,1)S(1)}, bf16[288,512]{1,0:T(8,128)(2,1)S(1)}, u32[]{:S(2)}, u32[]{:S(2)}) collective-permute-start(bf16[288,512]{1,0:T(8,128)(2,1)S(1)} %get-tuple-element.101), channel_id=1, source_target_pairs={{0,1},{1,0},{2,3},{3,2},{4,5},{5,4},{6,7},{7,6},{8,9},{9,8},{10,11... | collective-permute-start | bytes 884744 | tf_op jit(solution)/shard_map/send_home_0/ppermute | solution.py:298
  54.0 22.2 %collective-permute-start.22 = (bf16[288,512]{1,0:T(8,128)(2,1)S(1)}, bf16[288,512]{1,0:T(8,128)(2,1)S(1)}, u32[]{:S(2)}, u32[]{:S(2)}) collective-permute-start(bf16[288,512]{1,0:T(8,128)(2,1)S(1)} %get-tuple-element.102), channel_id=1, source_target_pairs={{0,2},{1,3},{2,0},{3,1},{4,6},{5,7},{6,4},{7,5},{8,10},{9,11},{10,... | collective-permute-start | bytes 884744 | tf_op jit(solution)/shard_map/send_home_0/ppermute | solution.py:298
  57.5 20.6 %collective-permute-start.23 = (bf16[288,512]{1,0:T(8,128)(2,1)S(1)}, bf16[288,512]{1,0:T(8,128)(2,1)S(1)}, u32[]{:S(2)}, u32[]{:S(2)}) collective-permute-start(bf16[288,512]{1,0:T(8,128)(2,1)S(1)} %get-tuple-element.103), channel_id=1, source_target_pairs={{0,3},{1,2},{2,1},{3,0},{4,7},{5,6},{6,5},{7,4},{8,11},{9,10},{10,... | collective-permute-start | bytes 884744 | tf_op jit(solution)/shard_map/send_home_0/ppermute | solution.py:298
  59.7 11.8 %collective-permute-start.9 = (bf16[4,288,256]{2,1,0:T(8,128)(2,1)S(1)}, bf16[4,288,256]{2,1,0:T(8,128)(2,1)S(1)}, u32[]{:S(2)}, u32[]{:S(2)}) collective-permute-start(bf16[4,288,256]{2,1,0:T(8,128)(2,1)S(1)} %get-tuple-element.82), channel_id=1, source_target_pairs={{4,0},{8,4},{12,8},{16,12},{20,16},{24,20},{28,24},{5,1},{9,5},{13... | collective-permute-start | bytes 1769480 | tf_op jit(solution)/shard_map/send_back_1/ppermute | solution.py:292
  62.6 9.6 %collective-permute-start.13 = (bf16[4,208,256]{2,1,0:T(8,128)(2,1)S(1)}, bf16[4,208,256]{2,1,0:T(8,128)(2,1)S(1)}, u32[]{:S(2)}, u32[]{:S(2)}) collective-permute-start(bf16[4,208,256]{2,1,0:T(8,128)(2,1)S(1)} %pad_maximum_fusion.2), channel_id=1, source_target_pairs={{0,4},{4,8},{8,12},{12,16},{16,20},{20,24},{24,28},{1,5},{5,9},{9,... | collective-permute-start | bytes 1277960 | tf_op jit(solution)/shard_map/send_next_2/ppermute | solution.py:292
  71.6 15.7 %collective-permute-start.18 = (bf16[288,512]{1,0:T(8,128)(2,1)S(1)}, bf16[288,512]{1,0:T(8,128)(2,1)S(1)}, u32[]{:S(2)}, u32[]{:S(2)}) collective-permute-start(bf16[288,512]{1,0:T(8,128)(2,1)S(1)} %get-tuple-element.98), channel_id=1, source_target_pairs={{0,1},{1,0},{2,3},{3,2},{4,5},{5,4},{6,7},{7,6},{8,9},{9,8},{10,11... | collective-permute-start | bytes 884744 | tf_op jit(solution)/shard_map/send_home_1/ppermute | solution.py:298
  72.2 16.1 %collective-permute-start.19 = (bf16[288,512]{1,0:T(8,128)(2,1)S(1)}, bf16[288,512]{1,0:T(8,128)(2,1)S(1)}, u32[]{:S(2)}, u32[]{:S(2)}) collective-permute-start(bf16[288,512]{1,0:T(8,128)(2,1)S(1)} %get-tuple-element.99), channel_id=1, source_target_pairs={{0,2},{1,3},{2,0},{3,1},{4,6},{5,7},{6,4},{7,5},{8,10},{9,11},{10,... | collective-permute-start | bytes 884744 | tf_op jit(solution)/shard_map/send_home_1/ppermute | solution.py:298
  74.9 13.4 %collective-permute-start.20 = (bf16[288,512]{1,0:T(8,128)(2,1)S(1)}, bf16[288,512]{1,0:T(8,128)(2,1)S(1)}, u32[]{:S(2)}, u32[]{:S(2)}) collective-permute-start(bf16[288,512]{1,0:T(8,128)(2,1)S(1)} %get-tuple-element.100), channel_id=1, source_target_pairs={{0,3},{1,2},{2,1},{3,0},{4,7},{5,6},{6,5},{7,4},{8,11},{9,10},{10,... | collective-permute-start | bytes 884744 | tf_op jit(solution)/shard_map/send_home_1/ppermute | solution.py:298
  76.1 9.4 %collective-permute-start.14 = (bf16[4,192,256]{2,1,0:T(8,128)(2,1)S(1)}, bf16[4,192,256]{2,1,0:T(8,128)(2,1)S(1)}, u32[]{:S(2)}, u32[]{:S(2)}) collective-permute-start(bf16[4,192,256]{2,1,0:T(8,128)(2,1)S(1)} %get-tuple-element.93), channel_id=1, source_target_pairs={{4,0},{8,4},{12,8},{16,12},{20,16},{24,20},{28,24},{5,1},{9,5},{13... | collective-permute-start | bytes 1179656 | tf_op jit(solution)/shard_map/send_back_2/ppermute | solution.py:292
  85.6 7.0 %collective-permute-start.15 = (bf16[192,512]{1,0:T(8,128)(2,1)S(1)}, bf16[192,512]{1,0:T(8,128)(2,1)S(1)}, u32[]{:S(2)}, u32[]{:S(2)}) collective-permute-start(bf16[192,512]{1,0:T(8,128)(2,1)S(1)} %get-tuple-element.95), channel_id=1, source_target_pairs={{0,1},{1,0},{2,3},{3,2},{4,5},{5,4},{6,7},{7,6},{8,9},{9,8},{10,11... | collective-permute-start | bytes 589832 | tf_op jit(solution)/shard_map/send_home_2/ppermute | solution.py:298
  86.1 9.2 %collective-permute-start.16 = (bf16[192,512]{1,0:T(8,128)(2,1)S(1)}, bf16[192,512]{1,0:T(8,128)(2,1)S(1)}, u32[]{:S(2)}, u32[]{:S(2)}) collective-permute-start(bf16[192,512]{1,0:T(8,128)(2,1)S(1)} %get-tuple-element.96), channel_id=1, source_target_pairs={{0,2},{1,3},{2,0},{3,1},{4,6},{5,7},{6,4},{7,5},{8,10},{9,11},{10,... | collective-permute-start | bytes 589832 | tf_op jit(solution)/shard_map/send_home_2/ppermute | solution.py:298
  87.3 9.0 %collective-permute-start.17 = (bf16[192,512]{1,0:T(8,128)(2,1)S(1)}, bf16[192,512]{1,0:T(8,128)(2,1)S(1)}, u32[]{:S(2)}, u32[]{:S(2)}) collective-permute-start(bf16[192,512]{1,0:T(8,128)(2,1)S(1)} %get-tuple-element.97), channel_id=1, source_target_pairs={{0,3},{1,2},{2,1},{3,0},{4,7},{5,6},{6,5},{7,4},{8,11},{9,10},{10,... | collective-permute-start | bytes 589832 | tf_op jit(solution)/shard_map/send_home_2/ppermute | solution.py:298
  (8 other events, 34.2 us)
